TPU v7x, 128 devices: a whole 4x4x4 slice. The times are simulated.
128 devices in a mesh: px: 8 (over x, core), py: 16 (over y, z).
Axes of the slice: x: 4, y: 4, z: 4, core: 2. Of those that a mesh axis runs over, the one named last changes fastest.
Arguments:
- modes_disp: bfloat16 [288, 262144], P(None, ('px', 'py')), may hold values from -6 to 6
- recovery: bfloat16 [24, 24, 262144], P(None, None, ('px', 'py')), may hold values from -1.25 to 1.25
- connect: int32 [4, 262144], P(None, ('px', 'py')), may hold values from 0 to 2047, as said below
- read_elem: int32 [65536], P(('px', 'py')), may hold values from 0 to 2047
- read_wts: float32 [24, 65536], P(None, ('px', 'py')), may hold values from -1.25 to 1.25
- zone: int32 [65536, 1], P(('px', 'py')), may hold values from 0 to 127; in each aligned block of 512 rows (0 to 511, 512 to 1023, ...) at most 8 rows name the same one
- response: bfloat16 [48, 576], replicated, may hold values from -0.875 to 0.875
Outputs:
- transfer: bfloat16 [131072, 576], P(('px', 'py'))
Inputs may be any that keep to these rules, and one draw needn't show every extreme that they name: `connect`: each partition's 2048 columns name every one of its 2048 nodes at least once. Among the read-out points of one partition no zone is named more than 8 times, a bound that some block reaches.
All inputs are finite; a program needn't handle non-finite values.
Results may differ from a plain program's by a relative error of at most 0.005.
Values may be sent and summed in bfloat16 or wider, within the bound.
No kernel may reach another device: no remote copies, remote signals or barrier semaphores. Data moves between devices by JAX's collectives and lax.ppermute only.
A program may use at most 64 MiB of HBM per device.

v0:
```python
import functools

import jax
import jax.numpy as jnp
from jax import lax
from jax.experimental import pallas as pl
from jax.experimental.pallas import tpu as pltpu
from jax.sharding import PartitionSpec as P

MODES = 48
CORNERS = 4
DOFS = 6
COMPS = 6
BORDER = 32
ROWS = COMPS * MODES
TALL = ROWS + 16
WIDE = 384
BLOCK = 256
TILE = 256
CHUNK = 512
LANES = 128
BF = jnp.bfloat16
F32 = jnp.float32


def hot(mask):
    return jnp.where(mask, jnp.ones((), BF), jnp.zeros((), BF))


def rows16(row):
    return jnp.broadcast_to(row, (16, row.shape[1])).astype(jnp.int16)


def tall16(row, count):
    width = row.shape[1]
    return jnp.broadcast_to(row[None], (count // 16, 16, width)).reshape(count, width)


def column_ids(connect_block):
    padded = jnp.concatenate([connect_block, connect_block], axis=0)
    turned = jnp.transpose(padded)
    parts = [
        jnp.broadcast_to(turned[:, c : c + 1], (BLOCK, LANES)).astype(jnp.int16)
        for c in range(CORNERS)
    ]
    return jnp.concatenate(parts, axis=0)


def stress_kernel(
    modes, recovery, connect, elems, acc, side_w, side_e, side_s, side_n, ids_out,
    rf, vn, vc, p_cur, p_prev, colb, qrow, accb,
):
    step = pl.program_id(0)
    steps = pl.num_programs(0)
    nodes = modes.shape[1]
    tiles = acc.shape[0]
    ones = jnp.ones((16, 2 * BLOCK), BF)

    def gather(corner, part, row):
        base = pl.multiple_of(part * CHUNK, CHUNK)
        ids = lax.broadcasted_iota(jnp.int16, (CHUNK, BLOCK), 0)
        mask = ids == tall16(rows16(row - base), CHUNK)
        return jnp.dot(modes[:, pl.ds(base, CHUNK)], hot(mask), preferred_element_type=F32)

    def scatter(tile, half):
        base = pl.multiple_of(half * 2 * BLOCK, 2 * BLOCK)
        lhs = jnp.concatenate(
            [
                p_prev[pl.ds(half * 2 * COMPS, COMPS)].reshape(ROWS, BLOCK),
                p_prev[pl.ds(half * 2 * COMPS + COMPS, COMPS)].reshape(ROWS, BLOCK),
            ],
            axis=1,
        )
        lhs = jnp.concatenate([lhs, ones], axis=0)
        ids = colb[pl.ds(base, 2 * BLOCK), :]
        mask = jnp.concatenate([ids, ids], axis=1) == tall16(qrow[tile], 2 * BLOCK)
        return jnp.dot(lhs, hot(mask), preferred_element_type=F32)

    @pl.when(step == 0)
    def _():
        ids = connect[...]
        high = lax.shift_right_logical(ids, 4)
        low = ids - high * 16
        split = jnp.concatenate([high, low], axis=0).astype(F32)
        split = jnp.concatenate([split, jnp.zeros_like(split)], axis=0).astype(BF)
        reads = elems.shape[1]
        got = jnp.zeros((16, reads), F32)
        for part in range(nodes // CHUNK):
            iota = lax.broadcasted_iota(jnp.int16, (CHUNK, reads), 0)
            mask = iota == tall16(rows16(elems[...] - part * CHUNK), CHUNK)
            got = got + jnp.dot(split[:, part * CHUNK : (part + 1) * CHUNK], hot(mask), preferred_element_type=F32)
        found = (got[0:4] * 16.0 + got[4:8]).astype(jnp.int32)
        ids_out[...] = found
        for tile in range(tiles):
            c, part = tile // (reads // TILE), tile % (reads // TILE)
            qrow[tile] = rows16(found[c : c + 1, part * TILE : (part + 1) * TILE])
        acc[...] = jnp.zeros_like(acc)
        accb[...] = jnp.zeros_like(accb)
        p_prev[...] = jnp.zeros_like(p_prev)
        colb[...] = jnp.full(colb.shape, -1, jnp.int16)

        for corner in range(CORNERS):
            row = connect[corner : corner + 1, 0:BLOCK]
            total = gather(corner, 0, row)
            for part in range(1, nodes // CHUNK):
                total = total + gather(corner, part, row)
            vc[corner] = total

    @pl.when(step > 0)
    def _():
        vc[...] = vn[...]

    vn[...] = jnp.zeros_like(vn)
    rf[...] = recovery[...].astype(F32)
    after = pl.multiple_of(jnp.minimum(step + 1, steps - 1) * BLOCK, BLOCK)

    @pl.loop(0, 16)
    def _(t):
        corner, part = t // 4, t % 4
        row = connect[pl.ds(corner, 1), pl.ds(after, BLOCK)]
        vn[corner] += gather(corner, part, row)
        acc[t % 8] += scatter(t % 8, t // 8)
        lanes = pl.ds(pl.multiple_of((t // 8) * LANES, LANES), LANES)
        first = (t % 8) * 3
        sums = [None] * 3
        for j in range(CORNERS * DOFS):
            moved = vc[j // DOFS, (j % DOFS) * MODES : (j % DOFS + 1) * MODES, lanes]
            for q in range(3):
                term = rf[first + q, j : j + 1, lanes] * moved
                sums[q] = term if j == 0 else sums[q] + term
        for q in range(3):
            p_cur[first + q, :, lanes] = sums[q].astype(BF)

    now = pl.multiple_of(step * BLOCK, BLOCK)
    p_prev[...] = p_cur[...]
    colb[...] = column_ids(connect[:, pl.ds(now, BLOCK)])
    lane_ids = lax.broadcasted_iota(jnp.int16, (2 * BLOCK, LANES), 1)
    for half in range(2):
        lhs = jnp.concatenate(
            [
                p_cur[half * 2 * COMPS + c * COMPS : half * 2 * COMPS + (c + 1) * COMPS].reshape(ROWS, BLOCK)
                for c in range(2)
            ],
            axis=1,
        )
        lhs = jnp.concatenate([lhs, ones], axis=0)
        mask = colb[half * 2 * BLOCK : (half + 1) * 2 * BLOCK, :] == lane_ids
        accb[...] += jnp.dot(lhs, hot(mask), preferred_element_type=F32)

    @pl.when(step == steps - 1)
    def _():
        tall = jnp.concatenate([accb[...], jnp.zeros((WIDE - TALL, LANES), F32)], axis=0)
        turned = jnp.transpose(tall)
        count = turned[:, ROWS : ROWS + 1].astype(jnp.int32)
        high = lax.shift_right_logical(count, 7)
        low = (count - high * 128).astype(F32)
        high = high.astype(F32)
        lane = lax.broadcasted_iota(jnp.int32, (LANES, WIDE), 1)
        out = jnp.where(lane < ROWS, turned, 0.0)
        out = jnp.where(lane == ROWS, high, out)
        out = jnp.where(lane == ROWS + 1, low, out).astype(BF)
        for side, ref in enumerate((side_w, side_e, side_s, side_n)):
            ref[...] = out[side * BORDER : (side + 1) * BORDER, :]

        @pl.loop(0, 16)
        def _(t):
            acc[t % 8] += scatter(t % 8, t // 8)


def readout_kernel(flags, acc, ids, got_w, got_e, got_s, got_n, weights, zone, out, *, zones, cap):
    reads = ids.shape[1]
    halves = reads // TILE
    pieces = []
    for side, ref in enumerate((got_w, got_e, got_s, got_n)):
        value = ref[...].astype(F32)
        pieces.append(jnp.where(flags[side] > 0, value, jnp.zeros_like(value)))
    border = jnp.transpose(jnp.concatenate(pieces, axis=0)).astype(BF)
    spots = [jnp.zeros((MODES, TILE), F32) for _ in range(halves)]
    iota = lax.broadcasted_iota(jnp.int32, (4 * BORDER, TILE), 0)
    for tile in range(acc.shape[0]):
        c, part = tile // halves, tile % halves
        at = slice(part * TILE, (part + 1) * TILE)
        mask = iota == ids[c : c + 1, at]
        more = jnp.dot(border, mask.astype(F32).astype(BF), preferred_element_type=F32)
        count = acc[tile, ROWS : ROWS + 1, :] + (more[ROWS : ROWS + 1] * 128.0 + more[ROWS + 1 : ROWS + 2])
        share = weights[c * COMPS : (c + 1) * COMPS, at] / count
        for k in range(COMPS):
            rows = slice(k * MODES, (k + 1) * MODES)
            spots[part] = spots[part] + share[k : k + 1] * (acc[tile, rows, :] + more[rows])
    spot = jnp.concatenate(spots, axis=1)
    spot = jnp.concatenate([spot, jnp.zeros((LANES - MODES, reads), F32)], axis=0)
    spot = jnp.transpose(spot).astype(BF)
    row = zone[...]
    column = jnp.transpose(jnp.broadcast_to(row, (8, reads)))[:, 0:1]
    at_row = lax.broadcasted_iota(jnp.int32, (reads, reads), 1)
    at_col = lax.broadcasted_iota(jnp.int32, (reads, reads), 0)
    same = jnp.where((column == row) & (at_col < at_row), 1.0, 0.0)
    rank = jnp.sum(same, axis=0, keepdims=True).astype(jnp.int32)
    slot = row * cap + rank
    chunk = 256
    for base in range(0, zones * cap, chunk):
        chosen = lax.broadcasted_iota(jnp.int32, (chunk, reads), 0) + base == slot
        out[base : base + chunk, :] = jnp.dot(
            chosen.astype(F32).astype(BF), spot, preferred_element_type=F32
        ).astype(BF)


def response_kernel(rows, response, out):
    out[...] = jnp.dot(rows[:, :MODES], response[...], preferred_element_type=F32).astype(BF)


def ring(x, axis, by):
    count = lax.axis_size(axis)
    return lax.ppermute(x, axis, [(i, (i + by) % count) for i in range(count)])


def params():
    return pltpu.CompilerParams(vmem_limit_bytes=56 * 2**20)


def per_device(modes_disp, recovery, connect, read_elem, read_wts, zone, response):
    elements = connect.shape[1]
    nodes = modes_disp.shape[1]
    reads = read_elem.shape[0]
    px, py = lax.axis_size("px"), lax.axis_size("py")
    zones = px * py
    cap = max(2, 2 * reads // zones)
    tiles = CORNERS * reads // TILE
    full = pl.BlockSpec(memory_space=pltpu.VMEM)
    side = jax.ShapeDtypeStruct((BORDER, WIDE), BF)
    whole = lambda *shape: pl.BlockSpec(shape, lambda i: (0,) * len(shape))
    acc, part_w, part_e, part_s, part_n, ids = pl.pallas_call(
        stress_kernel,
        grid=(elements // BLOCK,),
        in_specs=[
            whole(ROWS, nodes),
            pl.BlockSpec((CORNERS * COMPS, CORNERS * DOFS, BLOCK), lambda i: (0, 0, i)),
            whole(CORNERS, elements),
            whole(1, reads),
        ],
        out_specs=[whole(tiles, TALL, TILE)] + [whole(BORDER, WIDE)] * 4 + [whole(CORNERS, reads)],
        out_shape=[
            jax.ShapeDtypeStruct((tiles, TALL, TILE), F32),
            side, side, side, side,
            jax.ShapeDtypeStruct((CORNERS, reads), jnp.int32),
        ],
        scratch_shapes=[
            pltpu.VMEM((CORNERS * COMPS, CORNERS * DOFS, BLOCK), F32),
            pltpu.VMEM((CORNERS, ROWS, BLOCK), F32),
            pltpu.VMEM((CORNERS, ROWS, BLOCK), F32),
            pltpu.VMEM((CORNERS * COMPS, MODES, BLOCK), BF),
            pltpu.VMEM((CORNERS * COMPS, MODES, BLOCK), BF),
            pltpu.VMEM((CORNERS * BLOCK, LANES), jnp.int16),
            pltpu.VMEM((tiles, 16, TILE), jnp.int16),
            pltpu.VMEM((TALL, LANES), F32),
        ],
        compiler_params=params(),
        name="stress",
    )(modes_disp, recovery, connect, read_elem.reshape(1, reads))
    got_w = ring(part_e, "px", 1)
    got_e = ring(part_w, "px", -1)
    got_s = ring(part_n, "py", 1)
    got_n = ring(part_s, "py", -1)
    i, j = lax.axis_index("px"), lax.axis_index("py")
    flags = jnp.stack([i > 0, i < px - 1, j > 0, j < py - 1]).astype(jnp.int32)
    outgoing = pl.pallas_call(
        functools.partial(readout_kernel, zones=zones, cap=cap),
        in_specs=[pl.BlockSpec(memory_space=pltpu.SMEM)] + [full] * 8,
        out_specs=full,
        out_shape=jax.ShapeDtypeStruct((zones * cap, LANES), BF),
        compiler_params=params(),
        name="readout",
    )(flags, acc, ids, got_w, got_e, got_s, got_n, read_wts, zone.reshape(1, reads))
    arrived = lax.all_to_all(
        outgoing.reshape(zones, cap, LANES), ("px", "py"), split_axis=0, concat_axis=0, tiled=True
    ).reshape(zones * cap, LANES)
    cols = response.shape[1]
    split = 4
    return pl.pallas_call(
        response_kernel,
        grid=(split,),
        in_specs=[pl.BlockSpec((zones * cap // split, LANES), lambda i: (i, 0)), whole(MODES, cols)],
        out_specs=pl.BlockSpec((zones * cap // split, cols), lambda i: (i, 0)),
        out_shape=jax.ShapeDtypeStruct((zones * cap, cols), BF),
        compiler_params=params(),
        name="transfer",
    )(arrived, response)


def solution(mesh):
    placed = (
        P(None, ("px", "py")),
        P(None, None, ("px", "py")),
        P(None, ("px", "py")),
        P(("px", "py")),
        P(None, ("px", "py")),
        P(("px", "py"), None),
        P(),
    )
    return jax.shard_map(
        per_device, mesh=mesh, in_specs=placed, out_specs=P(("px", "py"), None), check_vma=False
    )
```

profile of v0, /device:TPU:1, one launch (start us, length us, event | category | flops | bytes accessed | tf_op | source)
XLA Modules:
  0.0 119.2 jit_solution(1133891671186253293)
XLA Ops:
  0.0 77.0 %stress.1 = (f32[8,304,256]{2,1,0:T(8,128)}, bf16[32,384]{1,0:T(8,128)(2,1)}, bf16[32,384]{1,0:T(8,128)(2,1)}, bf16[32,384]{1,0:T(8,128)(2,1)}, bf16[32,384]{1,0:T(8,128)(2,1)}, /*index=5*/s32[4,512]{1,0:T(4,128)}) custom-call(bf16[288,2048]{1,0:T(8,128)(2,1)} %modes.1, bf16[24,24,2048]{2,1,0:T(8,128)(2,1)} %recovery.1, s32[4,2048]{1,0:T(4,128)} %connect.1, ...), custom_call_target="tpu_custom_call" | custom-call | tf_op jit(solution)/shard_map/stress/pallas_call | solution.py:232
  77.0 2.6 %collective-permute-start = (bf16[32,384]{1,0:T(8,128)(2,1)}, bf16[32,384]{1,0:T(8,128)(2,1)S(1)}, u32[]{:S(2)}, u32[]{:S(2)}) collective-permute-start(bf16[32,384]{1,0:T(8,128)(2,1)} %get-tuple-element.13), channel_id=1, source_target_pairs={{0,16},{16,32},{32,48},{48,64},{64,80},{80,96},{96,112},{112,0},{1... | collective-permute-start | bytes 73736 | tf_op jit(solution)/shard_map/ppermute | solution.py:214
  79.6 0.0 collective-permute-start.1
  79.6 1.6 %collective-permute-start.2 = (bf16[32,384]{1,0:T(8,128)(2,1)}, bf16[32,384]{1,0:T(8,128)(2,1)S(1)}, u32[]{:S(2)}, u32[]{:S(2)}) collective-permute-start(bf16[32,384]{1,0:T(8,128)(2,1)} %get-tuple-element.15), channel_id=1, source_target_pairs={{0,1},{1,2},{2,3},{3,4},{4,5},{5,6},{6,7},{7,8},{8,9},{9,10},{10,1... | collective-permute-start | bytes 73736 | tf_op jit(solution)/shard_map/ppermute | solution.py:214
  81.2 4.6 %collective-permute-start.3 = (bf16[32,384]{1,0:T(8,128)(2,1)}, bf16[32,384]{1,0:T(8,128)(2,1)S(1)}, u32[]{:S(2)}, u32[]{:S(2)}) collective-permute-start(bf16[32,384]{1,0:T(8,128)(2,1)} %get-tuple-element.16), channel_id=1, source_target_pairs={{0,15},{1,0},{2,1},{3,2},{4,3},{5,4},{6,5},{7,6},{8,7},{9,8},{10,9... | collective-permute-start | bytes 73736 | tf_op jit(solution)/shard_map/ppermute | solution.py:214
  85.8 0.7 add_convert_fusion.flags
  86.5 0.0 collective-permute-done.got_w
  86.5 0.0 copy-start
  86.5 0.0 collective-permute-done.1.got_e
  86.5 0.0 copy-start.1
  86.5 0.7 collective-permute-done.2.got_s
  87.2 0.0 copy-start.2
  87.2 0.0 collective-permute-done.3.got_n
  87.2 0.0 copy-start.3
  87.2 0.0 copy-done
  87.2 0.0 copy-done.1
  87.3 0.6 copy-done.2
  87.8 0.0 copy-done.3
  87.9 3.9 %readout.1 = bf16[1024,128]{1,0:T(8,128)(2,1)} custom-call(s32[4]{0:T(128)} %add_convert_fusion.flags, f32[8,304,256]{2,1,0:T(8,128)} %get-tuple-element.11.acc, s32[4,512]{1,0:T(4,128)} %get-tuple-element.12.ids, bf16[32,384]{1,0:T(8,128)(2,1)} %copy-done, bf16[32,384]{1,0:T(8,128)(2,1)} %copy-done.1, bf16[32,384]{1,0:T(8,128)(2,1)} %copy-done.2, ...), custom_call_target="tpu_custom_call" | custom-call | tf_op jit(solution)/shard_map/readout/pallas_call | solution.py:266
  91.7 21.5 %all_to_all.5 = bf16[128,8,128]{2,1,0:T(8,128)(2,1)} all-to-all(bf16[128,8,128]{2,1,0:T(8,128)(2,1)} %bitcast.9), channel_id=1, replica_groups=mesh['px'=8,'py'=16] {'px','py'}, dimensions={0} | all-to-all | bytes 524288 | tf_op jit(solution)/shard_map/all_to_all | solution.py:274
  113.3 3.6 %transfer.1 = bf16[1024,576]{1,0:T(8,128)(2,1)} custom-call(bf16[1024,128]{1,0:T(8,128)(2,1)} %bitcast.8, bf16[48,576]{1,0:T(8,128)(2,1)} %response.1), custom_call_target="tpu_custom_call" | custom-call | tf_op jit(solution)/shard_map/transfer/pallas_call | solution.py:279
  116.9 2.4 %copy.8 = bf16[1024,576]{0,1:T(8,128)(2,1)} copy(bf16[1024,576]{1,0:T(8,128)(2,1)} %transfer.1) | data formatting | bytes 2359296 | tf_op jit(solution)/shard_map/transfer/pallas_call | solution.py:279
Async XLA Ops:
  77.0 9.5 %collective-permute-start = (bf16[32,384]{1,0:T(8,128)(2,1)}, bf16[32,384]{1,0:T(8,128)(2,1)S(1)}, u32[]{:S(2)}, u32[]{:S(2)}) collective-permute-start(bf16[32,384]{1,0:T(8,128)(2,1)} %get-tuple-element.13), channel_id=1, source_target_pairs={{0,16},{16,32},{32,48},{48,64},{64,80},{80,96},{96,112},{112,0},{1... | collective-permute-start | bytes 73736 | tf_op jit(solution)/shard_map/ppermute | solution.py:214
  79.6 6.9 %collective-permute-start.1 = (bf16[32,384]{1,0:T(8,128)(2,1)}, bf16[32,384]{1,0:T(8,128)(2,1)S(1)}, u32[]{:S(2)}, u32[]{:S(2)}) collective-permute-start(bf16[32,384]{1,0:T(8,128)(2,1)} %get-tuple-element.14), channel_id=1, source_target_pairs={{0,112},{16,0},{32,16},{48,32},{64,48},{80,64},{96,80},{112,96},{1... | collective-permute-start | bytes 73736 | tf_op jit(solution)/shard_map/ppermute | solution.py:214
  79.6 7.6 %collective-permute-start.2 = (bf16[32,384]{1,0:T(8,128)(2,1)}, bf16[32,384]{1,0:T(8,128)(2,1)S(1)}, u32[]{:S(2)}, u32[]{:S(2)}) collective-permute-start(bf16[32,384]{1,0:T(8,128)(2,1)} %get-tuple-element.15), channel_id=1, source_target_pairs={{0,1},{1,2},{2,3},{3,4},{4,5},{5,6},{6,7},{7,8},{8,9},{9,10},{10,1... | collective-permute-start | bytes 73736 | tf_op jit(solution)/shard_map/ppermute | solution.py:214
  81.2 6.0 %collective-permute-start.3 = (bf16[32,384]{1,0:T(8,128)(2,1)}, bf16[32,384]{1,0:T(8,128)(2,1)S(1)}, u32[]{:S(2)}, u32[]{:S(2)}) collective-permute-start(bf16[32,384]{1,0:T(8,128)(2,1)} %get-tuple-element.16), channel_id=1, source_target_pairs={{0,15},{1,0},{2,1},{3,2},{4,3},{5,4},{6,5},{7,6},{8,7},{9,8},{10,9... | collective-permute-start | bytes 73736 | tf_op jit(solution)/shard_map/ppermute | solution.py:214
  86.5 0.8 copy-start
  86.5 0.8 copy-start.1
  87.2 0.6 copy-start.2
  87.2 0.6 copy-start.3
where the time goes:
time: 120 us; the launch traced here: 119 us
  Pallas kernels  84.5 us (70%)
  blocking collectives  21.5 us (18%)
  starting transfers between devices  8.83 us (7%)
  local copies, waits for them, and re-layouts  2.98 us (2%)
    pallas_call x1, Pallas kernels, per_device(): pl.pallas_call(stress_kernel, grid=(elements // BLOCK,), in_specs=[whole(...  77 us
    all_to_all x1, blocking collectives, per_device(): lax.all_to_all(outgoing.reshape(zones, cap, LANES), ('px', 'py'), split_a...  21.5 us
    ppermute x4, starting transfers between devices, ring(): return lax.ppermute(x, axis, [(i, (i + by) % count) for i in range(count)])  8.83 us
    pallas_call x1, Pallas kernels, per_device(): pl.pallas_call(functools.partial(readout_kernel, zones=zones, cap=cap), i...  3.88 us
    pallas_call x1, Pallas kernels, per_device(): pl.pallas_call(response_kernel, grid=(split,), in_specs=[pl.BlockSpec((zo...  3.6 us
  transfers between devices with their start and end apart: 4, of which 1 were waited for; matrix products, arithmetic and copies ran while one was open for 1% of the time, Pallas kernels for 0%

commit v1 on v0

v1 whole, which is shorter than its diff:
```python
import functools

import jax
import jax.numpy as jnp
from jax import lax
from jax.experimental import pallas as pl
from jax.experimental.pallas import tpu as pltpu
from jax.sharding import PartitionSpec as P

MODES = 48
CORNERS = 4
DOFS = 6
COMPS = 6
BORDER = 32
ROWS = COMPS * MODES
TALL = ROWS + 16
WIDE = 384
BLOCK = 256
TILE = 256
GROUP = 12
STRIP = 16
LANES = 128
BF = jnp.bfloat16
F32 = jnp.float32


def hot(mask):
    return jnp.where(mask, jnp.ones((), BF), jnp.zeros((), BF))


def rows16(row):
    return jnp.broadcast_to(row, (16, row.shape[1])).astype(jnp.int16)


def tall16(row, count):
    width = row.shape[1]
    return jnp.broadcast_to(row[None], (count // 16, 16, width)).reshape(count, width)


def column_ids(connect_block):
    count = connect_block.shape[1]
    padded = jnp.concatenate([connect_block, connect_block], axis=0)
    turned = jnp.transpose(padded)
    parts = [
        jnp.broadcast_to(turned[:, c : c + 1], (count, LANES)).astype(jnp.int16)
        for c in range(CORNERS)
    ]
    return jnp.concatenate(parts, axis=0)


def with_ones(stress):
    count = stress.shape[2]
    sides = [stress[c * COMPS : (c + 1) * COMPS].reshape(ROWS, count) for c in range(CORNERS)]
    return jnp.concatenate(
        [jnp.concatenate(sides, axis=1), jnp.ones((TALL - ROWS, CORNERS * count), BF)], axis=0
    )


def stress_kernel(modes, recovery, connect, stress, side_w, side_e, side_s, side_n, rf, vc, accb):
    step = pl.program_id(0)
    nodes = modes.shape[1]

    @pl.when(step == 0)
    def _():
        accb[...] = jnp.zeros_like(accb)

    rf[...] = recovery[...].astype(F32)
    for corner in range(CORNERS):
        row = tall16(rows16(connect[corner : corner + 1, :]), nodes)
        ids = lax.broadcasted_iota(jnp.int16, (nodes, BLOCK), 0)
        vc[corner] = jnp.dot(modes[...], hot(ids == row), preferred_element_type=F32)

    for half in range(BLOCK // LANES):
        lanes = slice(half * LANES, (half + 1) * LANES)

        @pl.loop(0, CORNERS * COMPS // GROUP)
        def _(t):
            first = t * GROUP
            for part in range(MODES // STRIP):
                sums = [None] * GROUP
                for j in range(CORNERS * DOFS):
                    base = (j % DOFS) * MODES + part * STRIP
                    moved = vc[j // DOFS, base : base + STRIP, lanes]
                    for q in range(GROUP):
                        term = rf[first + q, j : j + 1, lanes] * moved
                        sums[q] = term if j == 0 else sums[q] + term
                for q in range(GROUP):
                    stress[first + q, part * STRIP : (part + 1) * STRIP, lanes] = sums[q].astype(BF)

    lane_ids = lax.broadcasted_iota(jnp.int16, (CORNERS * BLOCK, LANES), 1)
    mask = column_ids(connect[...]) == lane_ids
    accb[...] += jnp.dot(with_ones(stress[...]), hot(mask), preferred_element_type=F32)

    @pl.when(step == pl.num_programs(0) - 1)
    def _():
        tall = jnp.concatenate([accb[...], jnp.zeros((WIDE - TALL, LANES), F32)], axis=0)
        turned = jnp.transpose(tall)
        count = turned[:, ROWS : ROWS + 1].astype(jnp.int32)
        high = lax.shift_right_logical(count, 7)
        low = (count - high * 128).astype(F32)
        high = high.astype(F32)
        lane = lax.broadcasted_iota(jnp.int32, (LANES, WIDE), 1)
        out = jnp.where(lane < ROWS, turned, 0.0)
        out = jnp.where(lane == ROWS, high, out)
        out = jnp.where(lane == ROWS + 1, low, out).astype(BF)
        for side, ref in enumerate((side_w, side_e, side_s, side_n)):
            ref[...] = out[side * BORDER : (side + 1) * BORDER, :]


def weighted(values, shares, c, at):
    total = None
    for k in range(COMPS):
        term = shares[c * COMPS + k : c * COMPS + k + 1, at] * values[k * MODES : (k + 1) * MODES]
        total = term if k == 0 else total + term
    return total


def scatter_kernel(stress, connect, whole, elems, weights, spots, ids_out, colb, qrow, acc):
    step = pl.program_id(0)
    tiles = acc.shape[0]
    nodes = whole.shape[1]
    reads = elems.shape[1]
    halves = reads // TILE

    @pl.when(step == 0)
    def _():
        ids = whole[...]
        high = lax.shift_right_logical(ids, 4)
        low = ids - high * 16
        split = jnp.concatenate([high, low], axis=0).astype(F32)
        split = jnp.concatenate([split, jnp.zeros_like(split)], axis=0).astype(BF)
        iota = lax.broadcasted_iota(jnp.int16, (nodes, reads), 0)
        mask = iota == tall16(rows16(elems[...]), nodes)
        got = jnp.dot(split, hot(mask), preferred_element_type=F32)
        found = (got[0:4] * 16.0 + got[4:8]).astype(jnp.int32)
        ids_out[...] = found
        for tile in range(tiles):
            c, part = tile // halves, tile % halves
            qrow[tile] = rows16(found[c : c + 1, part * TILE : (part + 1) * TILE])
        acc[...] = jnp.zeros_like(acc)

    colb[...] = column_ids(connect[...])

    @pl.loop(0, tiles // 2)
    def _(t):
        lhs = with_ones(stress[...])
        ids = jnp.concatenate([colb[...], colb[...]], axis=1)
        for u in range(2):
            mask = ids == tall16(qrow[t * 2 + u], colb.shape[0])
            acc[t * 2 + u] += jnp.dot(lhs, hot(mask), preferred_element_type=F32)

    @pl.when(step == pl.num_programs(0) - 1)
    def _():
        for tile in range(tiles):
            c, part = tile // halves, tile % halves
            at = slice(part * TILE, (part + 1) * TILE)
            spots[c, 0:MODES, at] = weighted(acc[tile, 0:ROWS, :], weights, c, at)
            spots[c, MODES : MODES + 8, at] = acc[tile, ROWS : ROWS + 8, :]


def readout_kernel(flags, near, ids, got_w, got_e, got_s, got_n, weights, zone, out, *, zones, cap):
    reads = ids.shape[1]
    halves = reads // TILE
    pieces = []
    for side, ref in enumerate((got_w, got_e, got_s, got_n)):
        value = ref[...].astype(F32)
        pieces.append(jnp.where(flags[side] > 0, value, jnp.zeros_like(value)))
    border = jnp.transpose(jnp.concatenate(pieces, axis=0))[0:TALL].astype(BF)
    spots = [None] * halves
    iota = lax.broadcasted_iota(jnp.int32, (4 * BORDER, TILE), 0)
    for part in range(halves):
        at = slice(part * TILE, (part + 1) * TILE)
        for c in range(CORNERS):
            mask = iota == ids[c : c + 1, at]
            more = jnp.dot(border, mask.astype(F32).astype(BF), preferred_element_type=F32)
            count = near[c, MODES : MODES + 1, at] + (
                more[ROWS : ROWS + 1] * 128.0 + more[ROWS + 1 : ROWS + 2]
            )
            term = (near[c, 0:MODES, at] + weighted(more, weights, c, at)) / count
            spots[part] = term if c == 0 else spots[part] + term
    spot = jnp.concatenate(spots, axis=1)
    spot = jnp.concatenate([spot, jnp.zeros((LANES - MODES, reads), F32)], axis=0)
    spot = jnp.transpose(spot).astype(BF)
    row = zone[...]
    column = jnp.transpose(jnp.broadcast_to(row, (8, reads)))[:, 0:1]
    at_row = lax.broadcasted_iota(jnp.int32, (reads, reads), 1)
    at_col = lax.broadcasted_iota(jnp.int32, (reads, reads), 0)
    same = jnp.where((column == row) & (at_col < at_row), 1.0, 0.0)
    rank = jnp.sum(same, axis=0, keepdims=True).astype(jnp.int32)
    slot = row * cap + rank
    chunk = 256
    for base in range(0, zones * cap, chunk):
        chosen = lax.broadcasted_iota(jnp.int32, (chunk, reads), 0) + base == slot
        out[base : base + chunk, :] = jnp.dot(
            chosen.astype(F32).astype(BF), spot, preferred_element_type=F32
        ).astype(BF)


def response_kernel(rows, response, out):
    out[...] = lax.dot_general(
        response[...], rows[:, 0:MODES], (((0,), (1,)), ((), ())), preferred_element_type=F32
    ).astype(BF)


def ring(x, axis, by):
    count = lax.axis_size(axis)
    return lax.ppermute(x, axis, [(i, (i + by) % count) for i in range(count)])


def params():
    return pltpu.CompilerParams(vmem_limit_bytes=56 * 2**20)


def per_device(modes_disp, recovery, connect, read_elem, read_wts, zone, response):
    elements = connect.shape[1]
    nodes = modes_disp.shape[1]
    reads = read_elem.shape[0]
    px, py = lax.axis_size("px"), lax.axis_size("py")
    zones = px * py
    cap = max(2, 2 * reads // zones)
    tiles = CORNERS * reads // TILE
    full = pl.BlockSpec(memory_space=pltpu.VMEM)
    side = jax.ShapeDtypeStruct((BORDER, WIDE), BF)
    whole = lambda *shape: pl.BlockSpec(shape, lambda i: (0,) * len(shape))
    stress, part_w, part_e, part_s, part_n = pl.pallas_call(
        stress_kernel,
        grid=(elements // BLOCK,),
        in_specs=[
            whole(ROWS, nodes),
            pl.BlockSpec((CORNERS * COMPS, CORNERS * DOFS, BLOCK), lambda i: (0, 0, i)),
            pl.BlockSpec((CORNERS, BLOCK), lambda i: (0, i)),
        ],
        out_specs=[pl.BlockSpec((CORNERS * COMPS, MODES, BLOCK), lambda i: (0, 0, i))]
        + [whole(BORDER, WIDE)] * 4,
        out_shape=[
            jax.ShapeDtypeStruct((CORNERS * COMPS, MODES, elements), BF),
            side, side, side, side,
        ],
        scratch_shapes=[
            pltpu.VMEM((CORNERS * COMPS, CORNERS * DOFS, BLOCK), F32),
            pltpu.VMEM((CORNERS, ROWS, BLOCK), F32),
            pltpu.VMEM((TALL, LANES), F32),
        ],
        compiler_params=params(),
        cost_estimate=pl.CostEstimate(flops=10**10, bytes_accessed=10**7, transcendentals=0),
        name="stress",
    )(modes_disp, recovery, connect)
    got_w = ring(part_e, "px", 1)
    got_e = ring(part_w, "px", -1)
    got_s = ring(part_n, "py", 1)
    got_n = ring(part_s, "py", -1)
    big = 2 * BLOCK
    near, ids = pl.pallas_call(
        scatter_kernel,
        grid=(elements // big,),
        in_specs=[
            pl.BlockSpec((CORNERS * COMPS, MODES, big), lambda i: (0, 0, i)),
            pl.BlockSpec((CORNERS, big), lambda i: (0, i)),
            whole(CORNERS, elements),
            whole(1, reads),
            whole(CORNERS * COMPS, reads),
        ],
        out_specs=[whole(CORNERS, MODES + 8, reads), whole(CORNERS, reads)],
        out_shape=[
            jax.ShapeDtypeStruct((CORNERS, MODES + 8, reads), F32),
            jax.ShapeDtypeStruct((CORNERS, reads), jnp.int32),
        ],
        scratch_shapes=[
            pltpu.VMEM((CORNERS * big, LANES), jnp.int16),
            pltpu.VMEM((tiles, 16, TILE), jnp.int16),
            pltpu.VMEM((tiles, TALL, TILE), F32),
        ],
        compiler_params=params(),
        cost_estimate=pl.CostEstimate(flops=10**10, bytes_accessed=10**7, transcendentals=0),
        name="scatter",
    )(stress, connect, connect, read_elem.reshape(1, reads), read_wts)
    i, j = lax.axis_index("px"), lax.axis_index("py")
    flags = jnp.stack([i > 0, i < px - 1, j > 0, j < py - 1]).astype(jnp.int32)
    outgoing = pl.pallas_call(
        functools.partial(readout_kernel, zones=zones, cap=cap),
        in_specs=[pl.BlockSpec(memory_space=pltpu.SMEM)] + [full] * 8,
        out_specs=full,
        out_shape=jax.ShapeDtypeStruct((zones * cap, LANES), BF),
        compiler_params=params(),
        name="readout",
    )(flags, near, ids, got_w, got_e, got_s, got_n, read_wts, zone.reshape(1, reads))
    arrived = lax.all_to_all(
        outgoing.reshape(zones, cap, LANES), ("px", "py"), split_axis=0, concat_axis=0, tiled=True
    ).reshape(zones * cap, LANES)
    cols = response.shape[1]
    split = 4
    turned = pl.pallas_call(
        response_kernel,
        grid=(split,),
        in_specs=[pl.BlockSpec((zones * cap // split, LANES), lambda i: (i, 0)), whole(MODES, cols)],
        out_specs=pl.BlockSpec((cols, zones * cap // split), lambda i: (0, i)),
        out_shape=jax.ShapeDtypeStruct((cols, zones * cap), BF),
        compiler_params=params(),
        name="transfer",
    )(arrived, response)
    return jnp.transpose(turned)


def solution(mesh):
    placed = (
        P(None, ("px", "py")),
        P(None, None, ("px", "py")),
        P(None, ("px", "py")),
        P(("px", "py")),
        P(None, ("px", "py")),
        P(("px", "py"), None),
        P(),
    )
    return jax.shard_map(
        per_device, mesh=mesh, in_specs=placed, out_specs=P(("px", "py"), None), check_vma=False
    )
```

time: 120 us -> 88 us (0.73)
  Pallas kernels: 84.5 us -> 59.7 us
  blocking collectives: 21.5 us -> 17.8 us
  local copies, waits for them, and re-layouts: 2.98 us -> 0.59 us
    pallas_call x1, Pallas kernels: 77 us -> 35.3 us  [per_device(): pl.pallas_call(stress_kernel, grid=(elements // BLOCK,), in_specs=[whole(...]
    pallas_call x0 -> x1, Pallas kernels: none -> 17.8 us  [per_device(): pl.pallas_call(scatter_kernel, grid=(elements // big,), in_specs=[pl.Bloc...]
    all_to_all x1, blocking collectives: 21.5 us -> 17.8 us  [per_device(): lax.all_to_all(outgoing.reshape(zones, cap, LANES), ('px', 'py'), split_a...]
    pallas_call x1 -> x0, local copies, waits for them, and re-layouts: 2.37 us -> none  [per_device(): pl.pallas_call(response_kernel, grid=(split,), in_specs=[pl.BlockSpec((zo...]
  transfers between devices with their start and end apart: 4 -> 4, of which waited for: 1 -> 0; matrix products, arithmetic and copies ran while one was open for 1% -> 1% of each run, Pallas kernels for 0% -> 20%
where the time goes in v1:
time: 88 us; the launch traced here: 87.6 us
  Pallas kernels  59.7 us (68%)
  blocking collectives  17.8 us (20%)
  starting transfers between devices  8.81 us (10%)
    pallas_call x1, Pallas kernels, per_device(): pl.pallas_call(stress_kernel, grid=(elements // BLOCK,), in_specs=[whole(...  35.3 us
    pallas_call x1, Pallas kernels, per_device(): pl.pallas_call(scatter_kernel, grid=(elements // big,), in_specs=[pl.Bloc...  17.8 us
    all_to_all x1, blocking collectives, per_device(): lax.all_to_all(outgoing.reshape(zones, cap, LANES), ('px', 'py'), split_a...  17.8 us
    ppermute x4, starting transfers between devices, ring(): return lax.ppermute(x, axis, [(i, (i + by) % count) for i in range(count)])  8.81 us
    pallas_call x1, Pallas kernels, per_device(): pl.pallas_call(response_kernel, grid=(split,), in_specs=[pl.BlockSpec((zo...  3.66 us
    pallas_call x1, Pallas kernels, per_device(): pl.pallas_call(functools.partial(readout_kernel, zones=zones, cap=cap), i...  2.95 us
  transfers between devices with their start and end apart: 4, of which 0 were waited for; matrix products, arithmetic and copies ran while one was open for 1% of the time, Pallas kernels for 20%

profile of v1, /device:TPU:1, one launch (start us, length us, event | category | flops | bytes accessed | tf_op | source)
XLA Modules:
  0.0 87.6 jit_solution(8384301918834307717)
XLA Ops:
  0.0 35.3 %stress.1 = (bf16[24,48,2048]{2,1,0:T(8,128)(2,1)}, bf16[32,384]{1,0:T(8,128)(2,1)}, bf16[32,384]{1,0:T(8,128)(2,1)}, bf16[32,384]{1,0:T(8,128)(2,1)}, bf16[32,384]{1,0:T(8,128)(2,1)}) custom-call(bf16[288,2048]{1,0:T(8,128)(2,1)} %modes.1, bf16[24,24,2048]{2,1,0:T(8,128)(2,1)} %recovery.1, s32[4,2048]{1,0:T(4,128)} %whole.1), custom_call_target="tpu_custom_call" | custom-call | flops 10000000000 | bytes 10000000 | tf_op jit(solution)/shard_map/stress/pallas_call | solution.py:225
  35.3 2.6 %collective-permute-start = (bf16[32,384]{1,0:T(8,128)(2,1)}, bf16[32,384]{1,0:T(8,128)(2,1)S(1)}, u32[]{:S(2)}, u32[]{:S(2)}) collective-permute-start(bf16[32,384]{1,0:T(8,128)(2,1)} %get-tuple-element.15), channel_id=1, source_target_pairs={{0,16},{16,32},{32,48},{48,64},{64,80},{80,96},{96,112},{112,0},{1... | collective-permute-start | bytes 73736 | tf_op jit(solution)/shard_map/ppermute | solution.py:207
  37.9 0.0 collective-permute-start.1
  37.9 1.6 %collective-permute-start.2 = (bf16[32,384]{1,0:T(8,128)(2,1)}, bf16[32,384]{1,0:T(8,128)(2,1)S(1)}, u32[]{:S(2)}, u32[]{:S(2)}) collective-permute-start(bf16[32,384]{1,0:T(8,128)(2,1)} %get-tuple-element.17), channel_id=1, source_target_pairs={{0,1},{1,2},{2,3},{3,4},{4,5},{5,6},{6,7},{7,8},{8,9},{9,10},{10,1... | collective-permute-start | bytes 73736 | tf_op jit(solution)/shard_map/ppermute | solution.py:207
  39.5 4.6 %collective-permute-start.3 = (bf16[32,384]{1,0:T(8,128)(2,1)}, bf16[32,384]{1,0:T(8,128)(2,1)S(1)}, u32[]{:S(2)}, u32[]{:S(2)}) collective-permute-start(bf16[32,384]{1,0:T(8,128)(2,1)} %get-tuple-element.18), channel_id=1, source_target_pairs={{0,15},{1,0},{2,1},{3,2},{4,3},{5,4},{6,5},{7,6},{8,7},{9,8},{10,9... | collective-permute-start | bytes 73736 | tf_op jit(solution)/shard_map/ppermute | solution.py:207
  44.1 17.8 %scatter.1 = (f32[4,56,512]{2,1,0:T(8,128)}, s32[4,512]{1,0:T(4,128)}) custom-call(bf16[24,48,2048]{2,1,0:T(8,128)(2,1)} %get-tuple-element.12.stress, s32[4,2048]{1,0:T(4,128)} %whole.1, s32[4,2048]{1,0:T(4,128)} %whole.1, s32[1,512]{1,0:T(1,128)} %bitcast.12, f32[24,512]{1,0:T(8,128)} %weights.3), custom_call_target="tpu_custom_call" | custom-call | flops 10000000000 | bytes 10000000 | tf_op jit(solution)/shard_map/scatter/pallas_call | solution.py:253
  61.9 0.7 add_convert_fusion.flags
  62.6 0.0 collective-permute-done.got_w
  62.6 0.0 copy-start
  62.6 0.0 collective-permute-done.1.got_e
  62.6 0.0 copy-start.1
  62.6 0.0 collective-permute-done.2.got_s
  62.6 0.0 copy-start.2
  62.6 0.0 collective-permute-done.3.got_n
  62.6 0.0 copy-start.3
  62.6 0.5 copy-done
  63.2 0.0 copy-done.1
  63.2 0.0 copy-done.2
  63.2 0.0 copy-done.3
  63.2 3.0 %readout.1 = bf16[1024,128]{1,0:T(8,128)(2,1)} custom-call(s32[4]{0:T(128)} %add_convert_fusion.flags, f32[4,56,512]{2,1,0:T(8,128)} %get-tuple-element.13.near, s32[4,512]{1,0:T(4,128)} %get-tuple-element.14.ids, bf16[32,384]{1,0:T(8,128)(2,1)} %copy-done, bf16[32,384]{1,0:T(8,128)(2,1)} %copy-done.1, bf16[32,384]{1,0:T(8,128)(2,1)} %copy-done.2, ...), custom_call_target="tpu_custom_call" | custom-call | tf_op jit(solution)/shard_map/readout/pallas_call | solution.py:279
  66.2 17.8 %all_to_all.5 = bf16[128,8,128]{2,1,0:T(8,128)(2,1)} all-to-all(bf16[128,8,128]{2,1,0:T(8,128)(2,1)} %bitcast.9), channel_id=1, replica_groups=mesh['px'=8,'py'=16] {'px','py'}, dimensions={0} | all-to-all | bytes 524288 | tf_op jit(solution)/shard_map/all_to_all | solution.py:287
  84.0 3.7 %transfer.1 = bf16[576,1024]{1,0:T(8,128)(2,1)} custom-call(bf16[1024,128]{1,0:T(8,128)(2,1)} %bitcast.10, bf16[48,576]{1,0:T(8,128)(2,1)} %response.1), custom_call_target="tpu_custom_call" | custom-call | tf_op jit(solution)/shard_map/transfer/pallas_call | solution.py:292
Async XLA Ops:
  35.3 27.3 %collective-permute-start = (bf16[32,384]{1,0:T(8,128)(2,1)}, bf16[32,384]{1,0:T(8,128)(2,1)S(1)}, u32[]{:S(2)}, u32[]{:S(2)}) collective-permute-start(bf16[32,384]{1,0:T(8,128)(2,1)} %get-tuple-element.15), channel_id=1, source_target_pairs={{0,16},{16,32},{32,48},{48,64},{64,80},{80,96},{96,112},{112,0},{1... | collective-permute-start | bytes 73736 | tf_op jit(solution)/shard_map/ppermute | solution.py:207
  37.9 24.7 %collective-permute-start.1 = (bf16[32,384]{1,0:T(8,128)(2,1)}, bf16[32,384]{1,0:T(8,128)(2,1)S(1)}, u32[]{:S(2)}, u32[]{:S(2)}) collective-permute-start(bf16[32,384]{1,0:T(8,128)(2,1)} %get-tuple-element.16), channel_id=1, source_target_pairs={{0,112},{16,0},{32,16},{48,32},{64,48},{80,64},{96,80},{112,96},{1... | collective-permute-start | bytes 73736 | tf_op jit(solution)/shard_map/ppermute | solution.py:207
  37.9 24.7 %collective-permute-start.2 = (bf16[32,384]{1,0:T(8,128)(2,1)}, bf16[32,384]{1,0:T(8,128)(2,1)S(1)}, u32[]{:S(2)}, u32[]{:S(2)}) collective-permute-start(bf16[32,384]{1,0:T(8,128)(2,1)} %get-tuple-element.17), channel_id=1, source_target_pairs={{0,1},{1,2},{2,3},{3,4},{4,5},{5,6},{6,7},{7,8},{8,9},{9,10},{10,1... | collective-permute-start | bytes 73736 | tf_op jit(solution)/shard_map/ppermute | solution.py:207
  39.5 23.1 %collective-permute-start.3 = (bf16[32,384]{1,0:T(8,128)(2,1)}, bf16[32,384]{1,0:T(8,128)(2,1)S(1)}, u32[]{:S(2)}, u32[]{:S(2)}) collective-permute-start(bf16[32,384]{1,0:T(8,128)(2,1)} %get-tuple-element.18), channel_id=1, source_target_pairs={{0,15},{1,0},{2,1},{3,2},{4,3},{5,4},{6,5},{7,6},{8,7},{9,8},{10,9... | collective-permute-start | bytes 73736 | tf_op jit(solution)/shard_map/ppermute | solution.py:207
  62.6 0.6 copy-start
  62.6 0.6 copy-start.1
  62.6 0.6 copy-start.2
  62.6 0.6 copy-start.3

commit v2 on v1

--- a/solution.py
+++ b/solution.py
@@ -19,6 +19,7 @@
 TILE = 256
 GROUP = 12
 STRIP = 16
+UNROLL = 2
 LANES = 128
 BF = jnp.bfloat16
 F32 = jnp.float32
@@ -37,15 +38,12 @@
     return jnp.broadcast_to(row[None], (count // 16, 16, width)).reshape(count, width)
 
 
-def column_ids(connect_block):
-    count = connect_block.shape[1]
-    padded = jnp.concatenate([connect_block, connect_block], axis=0)
-    turned = jnp.transpose(padded)
-    parts = [
-        jnp.broadcast_to(turned[:, c : c + 1], (count, LANES)).astype(jnp.int16)
-        for c in range(CORNERS)
-    ]
-    return jnp.concatenate(parts, axis=0)
+def line16(connect):
+    return jnp.concatenate([rows16(connect[c : c + 1, :]) for c in range(CORNERS)], axis=1)
+
+
+def dot_rows(x, y):
+    return lax.dot_general(x, y, (((1,), (1,)), ((), ())), preferred_element_type=F32)
 
 
 def with_ones(stress):
@@ -87,9 +85,8 @@
                 for q in range(GROUP):
                     stress[first + q, part * STRIP : (part + 1) * STRIP, lanes] = sums[q].astype(BF)
 
-    lane_ids = lax.broadcasted_iota(jnp.int16, (CORNERS * BLOCK, LANES), 1)
-    mask = column_ids(connect[...]) == lane_ids
-    accb[...] += jnp.dot(with_ones(stress[...]), hot(mask), preferred_element_type=F32)
+    ids = lax.broadcasted_iota(jnp.int16, (LANES, CORNERS * BLOCK), 0)
+    accb[...] += dot_rows(with_ones(stress[...]), hot(ids == tall16(line16(connect), LANES)))
 
     @pl.when(step == pl.num_programs(0) - 1)
     def _():
@@ -115,7 +112,7 @@
     return total
 
 
-def scatter_kernel(stress, connect, whole, elems, weights, spots, ids_out, colb, qrow, acc):
+def scatter_kernel(stress, connect, whole, elems, weights, spots, ids_out, qcol, acc):
     step = pl.program_id(0)
     tiles = acc.shape[0]
     nodes = whole.shape[1]
@@ -134,20 +131,21 @@
         got = jnp.dot(split, hot(mask), preferred_element_type=F32)
         found = (got[0:4] * 16.0 + got[4:8]).astype(jnp.int32)
         ids_out[...] = found
+        turned = jnp.transpose(jnp.concatenate([found, found], axis=0))
         for tile in range(tiles):
             c, part = tile // halves, tile % halves
-            qrow[tile] = rows16(found[c : c + 1, part * TILE : (part + 1) * TILE])
+            column = turned[part * TILE : (part + 1) * TILE, c : c + 1]
+            qcol[tile] = jnp.broadcast_to(column, (TILE, LANES)).astype(jnp.int16)
         acc[...] = jnp.zeros_like(acc)
 
-    colb[...] = column_ids(connect[...])
-
-    @pl.loop(0, tiles // 2)
+    @pl.loop(0, tiles // UNROLL)
     def _(t):
         lhs = with_ones(stress[...])
-        ids = jnp.concatenate([colb[...], colb[...]], axis=1)
-        for u in range(2):
-            mask = ids == tall16(qrow[t * 2 + u], colb.shape[0])
-            acc[t * 2 + u] += jnp.dot(lhs, hot(mask), preferred_element_type=F32)
+        line = tall16(line16(connect), TILE)
+        for u in range(UNROLL):
+            ids = qcol[t * UNROLL + u]
+            mask = jnp.concatenate([ids] * (line.shape[1] // LANES), axis=1) == line
+            acc[t * UNROLL + u] += dot_rows(lhs, hot(mask))
 
     @pl.when(step == pl.num_programs(0) - 1)
     def _():
@@ -158,13 +156,15 @@
             spots[c, MODES : MODES + 8, at] = acc[tile, ROWS : ROWS + 8, :]
 
 
-def readout_kernel(flags, near, ids, got_w, got_e, got_s, got_n, weights, zone, out, *, zones, cap):
+def readout_kernel(near, ids, got_w, got_e, got_s, got_n, weights, zone, out, *, zones, cap):
     reads = ids.shape[1]
     halves = reads // TILE
+    i, j = lax.axis_index("px"), lax.axis_index("py")
+    flags = (i > 0, i < lax.axis_size("px") - 1, j > 0, j < lax.axis_size("py") - 1)
     pieces = []
     for side, ref in enumerate((got_w, got_e, got_s, got_n)):
         value = ref[...].astype(F32)
-        pieces.append(jnp.where(flags[side] > 0, value, jnp.zeros_like(value)))
+        pieces.append(jnp.where(flags[side], value, jnp.zeros_like(value)))
     border = jnp.transpose(jnp.concatenate(pieces, axis=0))[0:TALL].astype(BF)
     spots = [None] * halves
     iota = lax.broadcasted_iota(jnp.int32, (4 * BORDER, TILE), 0)
@@ -196,12 +196,6 @@
         ).astype(BF)
 
 
-def response_kernel(rows, response, out):
-    out[...] = lax.dot_general(
-        response[...], rows[:, 0:MODES], (((0,), (1,)), ((), ())), preferred_element_type=F32
-    ).astype(BF)
-
-
 def ring(x, axis, by):
     count = lax.axis_size(axis)
     return lax.ppermute(x, axis, [(i, (i + by) % count) for i in range(count)])
@@ -266,39 +260,26 @@
             jax.ShapeDtypeStruct((CORNERS, reads), jnp.int32),
         ],
         scratch_shapes=[
-            pltpu.VMEM((CORNERS * big, LANES), jnp.int16),
-            pltpu.VMEM((tiles, 16, TILE), jnp.int16),
+            pltpu.VMEM((tiles, TILE, LANES), jnp.int16),
             pltpu.VMEM((tiles, TALL, TILE), F32),
         ],
         compiler_params=params(),
         cost_estimate=pl.CostEstimate(flops=10**10, bytes_accessed=10**7, transcendentals=0),
         name="scatter",
     )(stress, connect, connect, read_elem.reshape(1, reads), read_wts)
-    i, j = lax.axis_index("px"), lax.axis_index("py")
-    flags = jnp.stack([i > 0, i < px - 1, j > 0, j < py - 1]).astype(jnp.int32)
     outgoing = pl.pallas_call(
         functools.partial(readout_kernel, zones=zones, cap=cap),
-        in_specs=[pl.BlockSpec(memory_space=pltpu.SMEM)] + [full] * 8,
+        in_specs=[full] * 8,
         out_specs=full,
         out_shape=jax.ShapeDtypeStruct((zones * cap, LANES), BF),
         compiler_params=params(),
         name="readout",
-    )(flags, near, ids, got_w, got_e, got_s, got_n, read_wts, zone.reshape(1, reads))
+    )(near, ids, got_w, got_e, got_s, got_n, read_wts, zone.reshape(1, reads))
     arrived = lax.all_to_all(
         outgoing.reshape(zones, cap, LANES), ("px", "py"), split_axis=0, concat_axis=0, tiled=True
     ).reshape(zones * cap, LANES)
-    cols = response.shape[1]
-    split = 4
-    turned = pl.pallas_call(
-        response_kernel,
-        grid=(split,),
-        in_specs=[pl.BlockSpec((zones * cap // split, LANES), lambda i: (i, 0)), whole(MODES, cols)],
-        out_specs=pl.BlockSpec((cols, zones * cap // split), lambda i: (0, i)),
-        out_shape=jax.ShapeDtypeStruct((cols, zones * cap), BF),
-        compiler_params=params(),
-        name="transfer",
-    )(arrived, response)
-    return jnp.transpose(turned)
+    deep = jnp.pad(response, ((0, LANES - MODES), (0, 0)))
+    return jnp.dot(arrived, deep, preferred_element_type=F32).astype(BF)
 
 
 def solution(mesh):

time: 88 us -> 82.9 us (0.942)
  Pallas kernels: 59.7 us -> 54 us
  matrix products: 0 us -> 1.53 us
    pallas_call x1 -> x0, Pallas kernels: 3.66 us -> none  [per_device(): pl.pallas_call(response_kernel, grid=(split,), in_specs=[pl.BlockSpec((zo...]
    dot_general x0 -> x1, matrix products: none -> 1.53 us  [per_device(): return jnp.dot(arrived, deep, preferred_element_type=F32).astype(BF)]
    pallas_call x1, Pallas kernels: 35.3 us -> 34.1 us  [per_device(): pl.pallas_call(stress_kernel, grid=(elements // BLOCK,), in_specs=[whole(...]
    pallas_call x1, Pallas kernels: 17.8 us -> 16.9 us  [per_device(): pl.pallas_call(scatter_kernel, grid=(elements // big,), in_specs=[pl.Bloc...]
  transfers between devices with their start and end apart: 4 -> 4, of which waited for: 0 -> 0; matrix products, arithmetic and copies ran while one was open for 1% -> 0% of each run, Pallas kernels for 20% -> 20%
where the time goes in v2:
time: 82.9 us; the launch traced here: 82.7 us
  Pallas kernels  54 us (65%)
  blocking collectives  17.7 us (21%)
  starting transfers between devices  8.82 us (11%)
  matrix products  1.53 us (2%)
    pallas_call x1, Pallas kernels, per_device(): pl.pallas_call(stress_kernel, grid=(elements // BLOCK,), in_specs=[whole(...  34.1 us
    all_to_all x1, blocking collectives, per_device(): lax.all_to_all(outgoing.reshape(zones, cap, LANES), ('px', 'py'), split_a...  17.7 us
    pallas_call x1, Pallas kernels, per_device(): pl.pallas_call(scatter_kernel, grid=(elements // big,), in_specs=[pl.Bloc...  16.9 us
    ppermute x4, starting transfers between devices, ring(): return lax.ppermute(x, axis, [(i, (i + by) % count) for i in range(count)])  8.82 us
    pallas_call x1, Pallas kernels, per_device(): pl.pallas_call(functools.partial(readout_kernel, zones=zones, cap=cap), i...  2.97 us
  transfers between devices with their start and end apart: 4, of which 0 were waited for; matrix products, arithmetic and copies ran while one was open for 0% of the time, Pallas kernels for 20%

profile of v2, /device:TPU:1, one launch (start us, length us, event | category | flops | bytes accessed | tf_op | source)
XLA Modules:
  0.0 82.7 jit_solution(9499247128524322559)
XLA Ops:
  0.0 34.1 %stress.1 = (bf16[24,48,2048]{2,1,0:T(8,128)(2,1)}, bf16[32,384]{1,0:T(8,128)(2,1)}, bf16[32,384]{1,0:T(8,128)(2,1)}, bf16[32,384]{1,0:T(8,128)(2,1)}, bf16[32,384]{1,0:T(8,128)(2,1)}) custom-call(bf16[288,2048]{1,0:T(8,128)(2,1)} %modes.1, bf16[24,24,2048]{2,1,0:T(8,128)(2,1)} %recovery.1, s32[4,2048]{1,0:T(4,128)} %whole.1), custom_call_target="tpu_custom_call" | custom-call | flops 10000000000 | bytes 10000000 | tf_op jit(solution)/shard_map/stress/pallas_call | solution.py:219
  34.1 2.6 %collective-permute-start = (bf16[32,384]{1,0:T(8,128)(2,1)}, bf16[32,384]{1,0:T(8,128)(2,1)S(1)}, u32[]{:S(2)}, u32[]{:S(2)}) collective-permute-start(bf16[32,384]{1,0:T(8,128)(2,1)} %get-tuple-element.15), channel_id=1, source_target_pairs={{0,16},{16,32},{32,48},{48,64},{64,80},{80,96},{96,112},{112,0},{1... | collective-permute-start | bytes 73736 | tf_op jit(solution)/shard_map/ppermute | solution.py:201
  36.7 0.0 collective-permute-start.1
  36.7 1.6 %collective-permute-start.2 = (bf16[32,384]{1,0:T(8,128)(2,1)}, bf16[32,384]{1,0:T(8,128)(2,1)S(1)}, u32[]{:S(2)}, u32[]{:S(2)}) collective-permute-start(bf16[32,384]{1,0:T(8,128)(2,1)} %get-tuple-element.17), channel_id=1, source_target_pairs={{0,1},{1,2},{2,3},{3,4},{4,5},{5,6},{6,7},{7,8},{8,9},{9,10},{10,1... | collective-permute-start | bytes 73736 | tf_op jit(solution)/shard_map/ppermute | solution.py:201
  38.3 4.6 %collective-permute-start.3 = (bf16[32,384]{1,0:T(8,128)(2,1)}, bf16[32,384]{1,0:T(8,128)(2,1)S(1)}, u32[]{:S(2)}, u32[]{:S(2)}) collective-permute-start(bf16[32,384]{1,0:T(8,128)(2,1)} %get-tuple-element.18), channel_id=1, source_target_pairs={{0,15},{1,0},{2,1},{3,2},{4,3},{5,4},{6,5},{7,6},{8,7},{9,8},{10,9... | collective-permute-start | bytes 73736 | tf_op jit(solution)/shard_map/ppermute | solution.py:201
  42.9 0.0 copy-start
  42.9 16.9 %scatter.1 = (f32[4,56,512]{2,1,0:T(8,128)}, s32[4,512]{1,0:T(4,128)}) custom-call(bf16[24,48,2048]{2,1,0:T(8,128)(2,1)} %get-tuple-element.12.stress, s32[4,2048]{1,0:T(4,128)} %whole.1, s32[4,2048]{1,0:T(4,128)} %whole.1, s32[1,512]{1,0:T(1,128)} %bitcast.8, f32[24,512]{1,0:T(8,128)} %weights.3), custom_call_target="tpu_custom_call" | custom-call | flops 10000000000 | bytes 10000000 | tf_op jit(solution)/shard_map/scatter/pallas_call | solution.py:247
  59.8 0.0 collective-permute-done.got_w
  59.8 0.0 copy-start.1
  59.8 0.0 collective-permute-done.1.got_e
  59.8 0.0 copy-start.2
  59.8 0.0 collective-permute-done.2.got_s
  59.8 0.0 copy-start.3
  59.9 0.0 collective-permute-done.3.got_n
  59.9 0.0 copy-start.4
  59.9 0.5 copy-done.1
  60.4 0.0 copy-done.2
  60.4 0.0 copy-done.3
  60.4 0.0 copy-done.4
  60.5 3.0 %readout.1 = bf16[1024,128]{1,0:T(8,128)(2,1)} custom-call(f32[4,56,512]{2,1,0:T(8,128)} %get-tuple-element.13.near, s32[4,512]{1,0:T(4,128)} %get-tuple-element.14.ids, bf16[32,384]{1,0:T(8,128)(2,1)} %copy-done.1, bf16[32,384]{1,0:T(8,128)(2,1)} %copy-done.2, bf16[32,384]{1,0:T(8,128)(2,1)} %copy-done.3, bf16[32,384]{1,0:T(8,128)(2,1)} %copy-done.4, ...), custom_call_target="tpu_custom_call" | custom-call | tf_op jit(solution)/shard_map/readout/pallas_call | solution.py:270
  63.5 17.7 %all_to_all.5 = bf16[128,8,128]{2,1,0:T(8,128)(2,1)S(1)} all-to-all(bf16[128,8,128]{2,1,0:T(8,128)(2,1)} %bitcast.6), channel_id=1, replica_groups=mesh['px'=8,'py'=16] {'px','py'}, dimensions={0} | all-to-all | bytes 524288 | tf_op jit(solution)/shard_map/all_to_all | solution.py:278
  81.2 0.0 copy-done
  81.2 1.5 %convolution_convert_fusion = bf16[1024,576]{0,1:T(8,128)(2,1)} fusion(bf16[128,8,128]{2,1,0:T(8,128)(2,1)S(1)} %all_to_all.5, bf16[48,576]{1,0:T(8,128)(2,1)S(1)} %copy-done), kind=kOutput, calls=%fused_computation | convolution fusion | flops 151584768 | bytes 1497088 | tf_op jit(solution)/shard_map/dot_general | solution.py:282
Async XLA Ops:
  34.1 25.7 %collective-permute-start = (bf16[32,384]{1,0:T(8,128)(2,1)}, bf16[32,384]{1,0:T(8,128)(2,1)S(1)}, u32[]{:S(2)}, u32[]{:S(2)}) collective-permute-start(bf16[32,384]{1,0:T(8,128)(2,1)} %get-tuple-element.15), channel_id=1, source_target_pairs={{0,16},{16,32},{32,48},{48,64},{64,80},{80,96},{96,112},{112,0},{1... | collective-permute-start | bytes 73736 | tf_op jit(solution)/shard_map/ppermute | solution.py:201
  36.7 23.1 %collective-permute-start.1 = (bf16[32,384]{1,0:T(8,128)(2,1)}, bf16[32,384]{1,0:T(8,128)(2,1)S(1)}, u32[]{:S(2)}, u32[]{:S(2)}) collective-permute-start(bf16[32,384]{1,0:T(8,128)(2,1)} %get-tuple-element.16), channel_id=1, source_target_pairs={{0,112},{16,0},{32,16},{48,32},{64,48},{80,64},{96,80},{112,96},{1... | collective-permute-start | bytes 73736 | tf_op jit(solution)/shard_map/ppermute | solution.py:201
  36.7 23.1 %collective-permute-start.2 = (bf16[32,384]{1,0:T(8,128)(2,1)}, bf16[32,384]{1,0:T(8,128)(2,1)S(1)}, u32[]{:S(2)}, u32[]{:S(2)}) collective-permute-start(bf16[32,384]{1,0:T(8,128)(2,1)} %get-tuple-element.17), channel_id=1, source_target_pairs={{0,1},{1,2},{2,3},{3,4},{4,5},{5,6},{6,7},{7,8},{8,9},{9,10},{10,1... | collective-permute-start | bytes 73736 | tf_op jit(solution)/shard_map/ppermute | solution.py:201
  38.3 21.5 %collective-permute-start.3 = (bf16[32,384]{1,0:T(8,128)(2,1)}, bf16[32,384]{1,0:T(8,128)(2,1)S(1)}, u32[]{:S(2)}, u32[]{:S(2)}) collective-permute-start(bf16[32,384]{1,0:T(8,128)(2,1)} %get-tuple-element.18), channel_id=1, source_target_pairs={{0,15},{1,0},{2,1},{3,2},{4,3},{5,4},{6,5},{7,6},{8,7},{9,8},{10,9... | collective-permute-start | bytes 73736 | tf_op jit(solution)/shard_map/ppermute | solution.py:201
  42.9 38.3 %copy-start = (bf16[48,576]{1,0:T(8,128)(2,1)S(1)}, bf16[48,576]{1,0:T(8,128)(2,1)}, u32[]{:S(2)}) copy-start(bf16[48,576]{1,0:T(8,128)(2,1)} %param.13) | copy-start | bytes 165892
  59.8 0.6 copy-start.1
  59.8 0.6 copy-start.2
  59.8 0.6 copy-start.3
  59.9 0.6 copy-start.4

commit v3 on v2

--- a/solution.py
+++ b/solution.py
@@ -19,7 +19,7 @@
 TILE = 256
 GROUP = 12
 STRIP = 16
-UNROLL = 2
+UNROLL = 4
 LANES = 128
 BF = jnp.bfloat16
 F32 = jnp.float32
@@ -75,15 +75,19 @@
         def _(t):
             first = t * GROUP
             for part in range(MODES // STRIP):
-                sums = [None] * GROUP
-                for j in range(CORNERS * DOFS):
-                    base = (j % DOFS) * MODES + part * STRIP
-                    moved = vc[j // DOFS, base : base + STRIP, lanes]
-                    for q in range(GROUP):
-                        term = rf[first + q, j : j + 1, lanes] * moved
-                        sums[q] = term if j == 0 else sums[q] + term
+                done = []
+                for thin in range(0, STRIP, 8):
+                    sums = [None] * GROUP
+                    for j in range(CORNERS * DOFS):
+                        base = (j % DOFS) * MODES + part * STRIP + thin
+                        moved = vc[j // DOFS, base : base + 8, lanes]
+                        for q in range(GROUP):
+                            term = rf[first + q, j : j + 1, lanes] * moved
+                            sums[q] = term if j == 0 else sums[q] + term
+                    done.append(sums)
                 for q in range(GROUP):
-                    stress[first + q, part * STRIP : (part + 1) * STRIP, lanes] = sums[q].astype(BF)
+                    both = jnp.concatenate([sums[q] for sums in done], axis=0)
+                    stress[first + q, part * STRIP : (part + 1) * STRIP, lanes] = both.astype(BF)
 
     ids = lax.broadcasted_iota(jnp.int16, (LANES, CORNERS * BLOCK), 0)
     accb[...] += dot_rows(with_ones(stress[...]), hot(ids == tall16(line16(connect), LANES)))

time: 82.9 us -> 81.3 us (0.981)
  Pallas kernels: 54 us -> 52.4 us
    pallas_call x1, Pallas kernels: 16.9 us -> 15.3 us  [per_device(): pl.pallas_call(scatter_kernel, grid=(elements // big,), in_specs=[pl.Bloc...]
  transfers between devices with their start and end apart: 4 -> 4, of which waited for: 0 -> 0; matrix products, arithmetic and copies ran while one was open for 0% -> 0% of each run, Pallas kernels for 20% -> 19%
where the time goes in v3:
time: 81.3 us; the launch traced here: 81.1 us
  Pallas kernels  52.4 us (64%)
  blocking collectives  17.7 us (22%)
  starting transfers between devices  8.82 us (11%)
  matrix products  1.53 us (2%)
    pallas_call x1, Pallas kernels, per_device(): pl.pallas_call(stress_kernel, grid=(elements // BLOCK,), in_specs=[whole(...  34.1 us
    all_to_all x1, blocking collectives, per_device(): lax.all_to_all(outgoing.reshape(zones, cap, LANES), ('px', 'py'), split_a...  17.7 us
    pallas_call x1, Pallas kernels, per_device(): pl.pallas_call(scatter_kernel, grid=(elements // big,), in_specs=[pl.Bloc...  15.3 us
    ppermute x4, starting transfers between devices, ring(): return lax.ppermute(x, axis, [(i, (i + by) % count) for i in range(count)])  8.82 us
    pallas_call x1, Pallas kernels, per_device(): pl.pallas_call(functools.partial(readout_kernel, zones=zones, cap=cap), i...  2.98 us
  transfers between devices with their start and end apart: 4, of which 0 were waited for; matrix products, arithmetic and copies ran while one was open for 0% of the time, Pallas kernels for 19%

profile of v3, /device:TPU:1, one launch (start us, length us, event | category | flops | bytes accessed | tf_op | source)
XLA Modules:
  0.0 81.1 jit_solution(15095065902145983956)
XLA Ops:
  0.0 34.1 %stress.1 = (bf16[24,48,2048]{2,1,0:T(8,128)(2,1)}, bf16[32,384]{1,0:T(8,128)(2,1)}, bf16[32,384]{1,0:T(8,128)(2,1)}, bf16[32,384]{1,0:T(8,128)(2,1)}, bf16[32,384]{1,0:T(8,128)(2,1)}) custom-call(bf16[288,2048]{1,0:T(8,128)(2,1)} %modes.1, bf16[24,24,2048]{2,1,0:T(8,128)(2,1)} %recovery.1, s32[4,2048]{1,0:T(4,128)} %whole.1), custom_call_target="tpu_custom_call" | custom-call | flops 10000000000 | bytes 10000000 | tf_op jit(solution)/shard_map/stress/pallas_call | solution.py:223
  34.1 2.6 %collective-permute-start = (bf16[32,384]{1,0:T(8,128)(2,1)}, bf16[32,384]{1,0:T(8,128)(2,1)S(1)}, u32[]{:S(2)}, u32[]{:S(2)}) collective-permute-start(bf16[32,384]{1,0:T(8,128)(2,1)} %get-tuple-element.15), channel_id=1, source_target_pairs={{0,16},{16,32},{32,48},{48,64},{64,80},{80,96},{96,112},{112,0},{1... | collective-permute-start | bytes 73736 | tf_op jit(solution)/shard_map/ppermute | solution.py:205
  36.7 0.0 collective-permute-start.1
  36.7 1.6 %collective-permute-start.2 = (bf16[32,384]{1,0:T(8,128)(2,1)}, bf16[32,384]{1,0:T(8,128)(2,1)S(1)}, u32[]{:S(2)}, u32[]{:S(2)}) collective-permute-start(bf16[32,384]{1,0:T(8,128)(2,1)} %get-tuple-element.17), channel_id=1, source_target_pairs={{0,1},{1,2},{2,3},{3,4},{4,5},{5,6},{6,7},{7,8},{8,9},{9,10},{10,1... | collective-permute-start | bytes 73736 | tf_op jit(solution)/shard_map/ppermute | solution.py:205
  38.3 4.6 %collective-permute-start.3 = (bf16[32,384]{1,0:T(8,128)(2,1)}, bf16[32,384]{1,0:T(8,128)(2,1)S(1)}, u32[]{:S(2)}, u32[]{:S(2)}) collective-permute-start(bf16[32,384]{1,0:T(8,128)(2,1)} %get-tuple-element.18), channel_id=1, source_target_pairs={{0,15},{1,0},{2,1},{3,2},{4,3},{5,4},{6,5},{7,6},{8,7},{9,8},{10,9... | collective-permute-start | bytes 73736 | tf_op jit(solution)/shard_map/ppermute | solution.py:205
  42.9 0.0 copy-start
  42.9 15.3 %scatter.1 = (f32[4,56,512]{2,1,0:T(8,128)}, s32[4,512]{1,0:T(4,128)}) custom-call(bf16[24,48,2048]{2,1,0:T(8,128)(2,1)} %get-tuple-element.12.stress, s32[4,2048]{1,0:T(4,128)} %whole.1, s32[4,2048]{1,0:T(4,128)} %whole.1, s32[1,512]{1,0:T(1,128)} %bitcast.8, f32[24,512]{1,0:T(8,128)} %weights.3), custom_call_target="tpu_custom_call" | custom-call | flops 10000000000 | bytes 10000000 | tf_op jit(solution)/shard_map/scatter/pallas_call | solution.py:251
  58.2 0.0 collective-permute-done.got_w
  58.2 0.0 copy-start.1
  58.2 0.0 collective-permute-done.1.got_e
  58.2 0.0 copy-start.2
  58.2 0.0 collective-permute-done.2.got_s
  58.2 0.0 copy-start.3
  58.3 0.0 collective-permute-done.3.got_n
  58.3 0.0 copy-start.4
  58.3 0.5 copy-done.1
  58.8 0.0 copy-done.2
  58.8 0.0 copy-done.3
  58.9 0.0 copy-done.4
  58.9 3.0 %readout.1 = bf16[1024,128]{1,0:T(8,128)(2,1)} custom-call(f32[4,56,512]{2,1,0:T(8,128)} %get-tuple-element.13.near, s32[4,512]{1,0:T(4,128)} %get-tuple-element.14.ids, bf16[32,384]{1,0:T(8,128)(2,1)} %copy-done.1, bf16[32,384]{1,0:T(8,128)(2,1)} %copy-done.2, bf16[32,384]{1,0:T(8,128)(2,1)} %copy-done.3, bf16[32,384]{1,0:T(8,128)(2,1)} %copy-done.4, ...), custom_call_target="tpu_custom_call" | custom-call | tf_op jit(solution)/shard_map/readout/pallas_call | solution.py:274
  61.9 17.7 %all_to_all.5 = bf16[128,8,128]{2,1,0:T(8,128)(2,1)S(1)} all-to-all(bf16[128,8,128]{2,1,0:T(8,128)(2,1)} %bitcast.6), channel_id=1, replica_groups=mesh['px'=8,'py'=16] {'px','py'}, dimensions={0} | all-to-all | bytes 524288 | tf_op jit(solution)/shard_map/all_to_all | solution.py:282
  79.6 0.0 copy-done
  79.6 1.5 %convolution_convert_fusion = bf16[1024,576]{0,1:T(8,128)(2,1)} fusion(bf16[128,8,128]{2,1,0:T(8,128)(2,1)S(1)} %all_to_all.5, bf16[48,576]{1,0:T(8,128)(2,1)S(1)} %copy-done), kind=kOutput, calls=%fused_computation | convolution fusion | flops 151584768 | bytes 1497088 | tf_op jit(solution)/shard_map/dot_general | solution.py:286
Async XLA Ops:
  34.1 24.1 %collective-permute-start = (bf16[32,384]{1,0:T(8,128)(2,1)}, bf16[32,384]{1,0:T(8,128)(2,1)S(1)}, u32[]{:S(2)}, u32[]{:S(2)}) collective-permute-start(bf16[32,384]{1,0:T(8,128)(2,1)} %get-tuple-element.15), channel_id=1, source_target_pairs={{0,16},{16,32},{32,48},{48,64},{64,80},{80,96},{96,112},{112,0},{1... | collective-permute-start | bytes 73736 | tf_op jit(solution)/shard_map/ppermute | solution.py:205
  36.7 21.5 %collective-permute-start.1 = (bf16[32,384]{1,0:T(8,128)(2,1)}, bf16[32,384]{1,0:T(8,128)(2,1)S(1)}, u32[]{:S(2)}, u32[]{:S(2)}) collective-permute-start(bf16[32,384]{1,0:T(8,128)(2,1)} %get-tuple-element.16), channel_id=1, source_target_pairs={{0,112},{16,0},{32,16},{48,32},{64,48},{80,64},{96,80},{112,96},{1... | collective-permute-start | bytes 73736 | tf_op jit(solution)/shard_map/ppermute | solution.py:205
  36.7 21.5 %collective-permute-start.2 = (bf16[32,384]{1,0:T(8,128)(2,1)}, bf16[32,384]{1,0:T(8,128)(2,1)S(1)}, u32[]{:S(2)}, u32[]{:S(2)}) collective-permute-start(bf16[32,384]{1,0:T(8,128)(2,1)} %get-tuple-element.17), channel_id=1, source_target_pairs={{0,1},{1,2},{2,3},{3,4},{4,5},{5,6},{6,7},{7,8},{8,9},{9,10},{10,1... | collective-permute-start | bytes 73736 | tf_op jit(solution)/shard_map/ppermute | solution.py:205
  38.3 19.9 %collective-permute-start.3 = (bf16[32,384]{1,0:T(8,128)(2,1)}, bf16[32,384]{1,0:T(8,128)(2,1)S(1)}, u32[]{:S(2)}, u32[]{:S(2)}) collective-permute-start(bf16[32,384]{1,0:T(8,128)(2,1)} %get-tuple-element.18), channel_id=1, source_target_pairs={{0,15},{1,0},{2,1},{3,2},{4,3},{5,4},{6,5},{7,6},{8,7},{9,8},{10,9... | collective-permute-start | bytes 73736 | tf_op jit(solution)/shard_map/ppermute | solution.py:205
  42.9 36.7 %copy-start = (bf16[48,576]{1,0:T(8,128)(2,1)S(1)}, bf16[48,576]{1,0:T(8,128)(2,1)}, u32[]{:S(2)}) copy-start(bf16[48,576]{1,0:T(8,128)(2,1)} %param.13) | copy-start | bytes 165892
  58.2 0.6 copy-start.1
  58.2 0.6 copy-start.2
  58.2 0.6 copy-start.3
  58.3 0.6 copy-start.4

commit v4 on v3

--- a/solution.py
+++ b/solution.py
@@ -19,7 +19,7 @@
 TILE = 256
 GROUP = 12
 STRIP = 16
-UNROLL = 4
+UNROLL = 8
 LANES = 128
 BF = jnp.bfloat16
 F32 = jnp.float32
@@ -62,13 +62,17 @@
     def _():
         accb[...] = jnp.zeros_like(accb)
 
-    rf[...] = recovery[...].astype(F32)
+    halves = BLOCK // LANES
+    for half in range(halves):
+        rf[half] = recovery[:, :, half * LANES : (half + 1) * LANES].astype(F32)
     for corner in range(CORNERS):
         row = tall16(rows16(connect[corner : corner + 1, :]), nodes)
         ids = lax.broadcasted_iota(jnp.int16, (nodes, BLOCK), 0)
-        vc[corner] = jnp.dot(modes[...], hot(ids == row), preferred_element_type=F32)
-
-    for half in range(BLOCK // LANES):
+        moved = jnp.dot(modes[...], hot(ids == row), preferred_element_type=F32)
+        for half in range(halves):
+            vc[half, corner] = moved[:, half * LANES : (half + 1) * LANES]
+
+    for half in range(halves):
         lanes = slice(half * LANES, (half + 1) * LANES)
 
         @pl.loop(0, CORNERS * COMPS // GROUP)
@@ -80,9 +84,9 @@
                     sums = [None] * GROUP
                     for j in range(CORNERS * DOFS):
                         base = (j % DOFS) * MODES + part * STRIP + thin
-                        moved = vc[j // DOFS, base : base + 8, lanes]
+                        moved = vc[half, j // DOFS, base : base + 8, :]
                         for q in range(GROUP):
-                            term = rf[first + q, j : j + 1, lanes] * moved
+                            term = rf[half, first + q, j : j + 1, :] * moved
                             sums[q] = term if j == 0 else sums[q] + term
                     done.append(sums)
                 for q in range(GROUP):
@@ -235,8 +239,8 @@
             side, side, side, side,
         ],
         scratch_shapes=[
-            pltpu.VMEM((CORNERS * COMPS, CORNERS * DOFS, BLOCK), F32),
-            pltpu.VMEM((CORNERS, ROWS, BLOCK), F32),
+            pltpu.VMEM((BLOCK // LANES, CORNERS * COMPS, CORNERS * DOFS, LANES), F32),
+            pltpu.VMEM((BLOCK // LANES, CORNERS, ROWS, LANES), F32),
             pltpu.VMEM((TALL, LANES), F32),
         ],
         compiler_params=params(),

time: 81.3 us -> 78.5 us (0.966)
  Pallas kernels: 52.4 us -> 49.5 us
    pallas_call x1, Pallas kernels: 34.1 us -> 32.1 us  [per_device(): pl.pallas_call(stress_kernel, grid=(elements // BLOCK,), in_specs=[whole(...]
    pallas_call x1, Pallas kernels: 15.3 us -> 14.5 us  [per_device(): pl.pallas_call(scatter_kernel, grid=(elements // big,), in_specs=[pl.Bloc...]
  transfers between devices with their start and end apart: 4 -> 4, of which waited for: 0 -> 0; matrix products, arithmetic and copies ran while one was open for 0% -> 0% of each run, Pallas kernels for 19% -> 18%
where the time goes in v4:
time: 78.5 us; the launch traced here: 78.3 us
  Pallas kernels  49.5 us (63%)
  blocking collectives  17.7 us (23%)
  starting transfers between devices  8.82 us (11%)
  matrix products  1.53 us (2%)
    pallas_call x1, Pallas kernels, per_device(): pl.pallas_call(stress_kernel, grid=(elements // BLOCK,), in_specs=[whole(...  32.1 us
    all_to_all x1, blocking collectives, per_device(): lax.all_to_all(outgoing.reshape(zones, cap, LANES), ('px', 'py'), split_a...  17.7 us
    pallas_call x1, Pallas kernels, per_device(): pl.pallas_call(scatter_kernel, grid=(elements // big,), in_specs=[pl.Bloc...  14.5 us
    ppermute x4, starting transfers between devices, ring(): return lax.ppermute(x, axis, [(i, (i + by) % count) for i in range(count)])  8.82 us
    pallas_call x1, Pallas kernels, per_device(): pl.pallas_call(functools.partial(readout_kernel, zones=zones, cap=cap), i...  2.97 us
  transfers between devices with their start and end apart: 4, of which 0 were waited for; matrix products, arithmetic and copies ran while one was open for 0% of the time, Pallas kernels for 18%

profile of v4, /device:TPU:1, one launch (start us, length us, event | category | flops | bytes accessed | tf_op | source)
XLA Modules:
  0.0 78.3 jit_solution(15143568292843662488)
XLA Ops:
  0.0 32.1 %stress.1 = (bf16[24,48,2048]{2,1,0:T(8,128)(2,1)}, bf16[32,384]{1,0:T(8,128)(2,1)}, bf16[32,384]{1,0:T(8,128)(2,1)}, bf16[32,384]{1,0:T(8,128)(2,1)}, bf16[32,384]{1,0:T(8,128)(2,1)}) custom-call(bf16[288,2048]{1,0:T(8,128)(2,1)} %modes.1, bf16[24,24,2048]{2,1,0:T(8,128)(2,1)} %recovery.1, s32[4,2048]{1,0:T(4,128)} %whole.1), custom_call_target="tpu_custom_call" | custom-call | flops 10000000000 | bytes 10000000 | tf_op jit(solution)/shard_map/stress/pallas_call | solution.py:227
  32.1 2.6 %collective-permute-start = (bf16[32,384]{1,0:T(8,128)(2,1)}, bf16[32,384]{1,0:T(8,128)(2,1)S(1)}, u32[]{:S(2)}, u32[]{:S(2)}) collective-permute-start(bf16[32,384]{1,0:T(8,128)(2,1)} %get-tuple-element.15), channel_id=1, source_target_pairs={{0,16},{16,32},{32,48},{48,64},{64,80},{80,96},{96,112},{112,0},{1... | collective-permute-start | bytes 73736 | tf_op jit(solution)/shard_map/ppermute | solution.py:209
  34.7 0.0 collective-permute-start.1
  34.7 1.6 %collective-permute-start.2 = (bf16[32,384]{1,0:T(8,128)(2,1)}, bf16[32,384]{1,0:T(8,128)(2,1)S(1)}, u32[]{:S(2)}, u32[]{:S(2)}) collective-permute-start(bf16[32,384]{1,0:T(8,128)(2,1)} %get-tuple-element.17), channel_id=1, source_target_pairs={{0,1},{1,2},{2,3},{3,4},{4,5},{5,6},{6,7},{7,8},{8,9},{9,10},{10,1... | collective-permute-start | bytes 73736 | tf_op jit(solution)/shard_map/ppermute | solution.py:209
  36.4 4.6 %collective-permute-start.3 = (bf16[32,384]{1,0:T(8,128)(2,1)}, bf16[32,384]{1,0:T(8,128)(2,1)S(1)}, u32[]{:S(2)}, u32[]{:S(2)}) collective-permute-start(bf16[32,384]{1,0:T(8,128)(2,1)} %get-tuple-element.18), channel_id=1, source_target_pairs={{0,15},{1,0},{2,1},{3,2},{4,3},{5,4},{6,5},{7,6},{8,7},{9,8},{10,9... | collective-permute-start | bytes 73736 | tf_op jit(solution)/shard_map/ppermute | solution.py:209
  40.9 0.0 copy-start
  40.9 14.5 %scatter.1 = (f32[4,56,512]{2,1,0:T(8,128)}, s32[4,512]{1,0:T(4,128)}) custom-call(bf16[24,48,2048]{2,1,0:T(8,128)(2,1)} %get-tuple-element.12.stress, s32[4,2048]{1,0:T(4,128)} %whole.1, s32[4,2048]{1,0:T(4,128)} %whole.1, s32[1,512]{1,0:T(1,128)} %bitcast.8, f32[24,512]{1,0:T(8,128)} %weights.3), custom_call_target="tpu_custom_call" | custom-call | flops 10000000000 | bytes 10000000 | tf_op jit(solution)/shard_map/scatter/pallas_call | solution.py:255
  55.4 0.0 collective-permute-done.got_w
  55.4 0.0 copy-start.1
  55.4 0.0 collective-permute-done.1.got_e
  55.4 0.0 copy-start.2
  55.4 0.0 collective-permute-done.2.got_s
  55.4 0.0 copy-start.3
  55.4 0.0 collective-permute-done.3.got_n
  55.4 0.0 copy-start.4
  55.5 0.5 copy-done.1
  56.0 0.0 copy-done.2
  56.0 0.0 copy-done.3
  56.0 0.0 copy-done.4
  56.1 3.0 %readout.1 = bf16[1024,128]{1,0:T(8,128)(2,1)} custom-call(f32[4,56,512]{2,1,0:T(8,128)} %get-tuple-element.13.near, s32[4,512]{1,0:T(4,128)} %get-tuple-element.14.ids, bf16[32,384]{1,0:T(8,128)(2,1)} %copy-done.1, bf16[32,384]{1,0:T(8,128)(2,1)} %copy-done.2, bf16[32,384]{1,0:T(8,128)(2,1)} %copy-done.3, bf16[32,384]{1,0:T(8,128)(2,1)} %copy-done.4, ...), custom_call_target="tpu_custom_call" | custom-call | tf_op jit(solution)/shard_map/readout/pallas_call | solution.py:278
  59.0 17.7 %all_to_all.5 = bf16[128,8,128]{2,1,0:T(8,128)(2,1)S(1)} all-to-all(bf16[128,8,128]{2,1,0:T(8,128)(2,1)} %bitcast.6), channel_id=1, replica_groups=mesh['px'=8,'py'=16] {'px','py'}, dimensions={0} | all-to-all | bytes 524288 | tf_op jit(solution)/shard_map/all_to_all | solution.py:286
  76.7 0.0 copy-done
  76.7 1.5 %convolution_convert_fusion = bf16[1024,576]{0,1:T(8,128)(2,1)} fusion(bf16[128,8,128]{2,1,0:T(8,128)(2,1)S(1)} %all_to_all.5, bf16[48,576]{1,0:T(8,128)(2,1)S(1)} %copy-done), kind=kOutput, calls=%fused_computation | convolution fusion | flops 151584768 | bytes 1497088 | tf_op jit(solution)/shard_map/dot_general | solution.py:290
Async XLA Ops:
  32.1 23.3 %collective-permute-start = (bf16[32,384]{1,0:T(8,128)(2,1)}, bf16[32,384]{1,0:T(8,128)(2,1)S(1)}, u32[]{:S(2)}, u32[]{:S(2)}) collective-permute-start(bf16[32,384]{1,0:T(8,128)(2,1)} %get-tuple-element.15), channel_id=1, source_target_pairs={{0,16},{16,32},{32,48},{48,64},{64,80},{80,96},{96,112},{112,0},{1... | collective-permute-start | bytes 73736 | tf_op jit(solution)/shard_map/ppermute | solution.py:209
  34.7 20.7 %collective-permute-start.1 = (bf16[32,384]{1,0:T(8,128)(2,1)}, bf16[32,384]{1,0:T(8,128)(2,1)S(1)}, u32[]{:S(2)}, u32[]{:S(2)}) collective-permute-start(bf16[32,384]{1,0:T(8,128)(2,1)} %get-tuple-element.16), channel_id=1, source_target_pairs={{0,112},{16,0},{32,16},{48,32},{64,48},{80,64},{96,80},{112,96},{1... | collective-permute-start | bytes 73736 | tf_op jit(solution)/shard_map/ppermute | solution.py:209
  34.7 20.7 %collective-permute-start.2 = (bf16[32,384]{1,0:T(8,128)(2,1)}, bf16[32,384]{1,0:T(8,128)(2,1)S(1)}, u32[]{:S(2)}, u32[]{:S(2)}) collective-permute-start(bf16[32,384]{1,0:T(8,128)(2,1)} %get-tuple-element.17), channel_id=1, source_target_pairs={{0,1},{1,2},{2,3},{3,4},{4,5},{5,6},{6,7},{7,8},{8,9},{9,10},{10,1... | collective-permute-start | bytes 73736 | tf_op jit(solution)/shard_map/ppermute | solution.py:209
  36.4 19.1 %collective-permute-start.3 = (bf16[32,384]{1,0:T(8,128)(2,1)}, bf16[32,384]{1,0:T(8,128)(2,1)S(1)}, u32[]{:S(2)}, u32[]{:S(2)}) collective-permute-start(bf16[32,384]{1,0:T(8,128)(2,1)} %get-tuple-element.18), channel_id=1, source_target_pairs={{0,15},{1,0},{2,1},{3,2},{4,3},{5,4},{6,5},{7,6},{8,7},{9,8},{10,9... | collective-permute-start | bytes 73736 | tf_op jit(solution)/shard_map/ppermute | solution.py:209
  40.9 35.8 %copy-start = (bf16[48,576]{1,0:T(8,128)(2,1)S(1)}, bf16[48,576]{1,0:T(8,128)(2,1)}, u32[]{:S(2)}) copy-start(bf16[48,576]{1,0:T(8,128)(2,1)} %param.13) | copy-start | bytes 165892
  55.4 0.6 copy-start.1
  55.4 0.6 copy-start.2
  55.4 0.6 copy-start.3
  55.4 0.6 copy-start.4

commit v5 on v4

--- a/solution.py
+++ b/solution.py
@@ -15,7 +15,7 @@
 ROWS = COMPS * MODES
 TALL = ROWS + 16
 WIDE = 384
-BLOCK = 256
+BLOCK = 512
 TILE = 256
 GROUP = 12
 STRIP = 16
@@ -251,7 +251,7 @@
     got_e = ring(part_w, "px", -1)
     got_s = ring(part_n, "py", 1)
     got_n = ring(part_s, "py", -1)
-    big = 2 * BLOCK
+    big = BLOCK
     near, ids = pl.pallas_call(
         scatter_kernel,
         grid=(elements // big,),

time: 78.5 us -> 77.5 us (0.987)
  Pallas kernels: 49.5 us -> 48.5 us
    pallas_call x1, Pallas kernels: 32.1 us -> 31.1 us  [per_device(): pl.pallas_call(stress_kernel, grid=(elements // BLOCK,), in_specs=[whole(...]
  transfers between devices with their start and end apart: 4 -> 4, of which waited for: 0 -> 0; matrix products, arithmetic and copies ran while one was open for 0% -> 0% of each run, Pallas kernels for 18% -> 19%
where the time goes in v5:
time: 77.5 us; the launch traced here: 77.2 us
  Pallas kernels  48.5 us (63%)
  blocking collectives  17.7 us (23%)
  starting transfers between devices  8.83 us (11%)
  matrix products  1.53 us (2%)
    pallas_call x1, Pallas kernels, per_device(): pl.pallas_call(stress_kernel, grid=(elements // BLOCK,), in_specs=[whole(...  31.1 us
    all_to_all x1, blocking collectives, per_device(): lax.all_to_all(outgoing.reshape(zones, cap, LANES), ('px', 'py'), split_a...  17.7 us
    pallas_call x1, Pallas kernels, per_device(): pl.pallas_call(scatter_kernel, grid=(elements // big,), in_specs=[pl.Bloc...  14.5 us
    ppermute x4, starting transfers between devices, ring(): return lax.ppermute(x, axis, [(i, (i + by) % count) for i in range(count)])  8.83 us
    pallas_call x1, Pallas kernels, per_device(): pl.pallas_call(functools.partial(readout_kernel, zones=zones, cap=cap), i...  2.98 us
  transfers between devices with their start and end apart: 4, of which 0 were waited for; matrix products, arithmetic and copies ran while one was open for 0% of the time, Pallas kernels for 19%

profile of v5, /device:TPU:1, one launch (start us, length us, event | category | flops | bytes accessed | tf_op | source)
XLA Modules:
  0.0 77.2 jit_solution(2769030872634426218)
XLA Ops:
  0.0 31.1 %stress.1 = (bf16[24,48,2048]{2,1,0:T(8,128)(2,1)}, bf16[32,384]{1,0:T(8,128)(2,1)}, bf16[32,384]{1,0:T(8,128)(2,1)}, bf16[32,384]{1,0:T(8,128)(2,1)}, bf16[32,384]{1,0:T(8,128)(2,1)}) custom-call(bf16[288,2048]{1,0:T(8,128)(2,1)} %modes.1, bf16[24,24,2048]{2,1,0:T(8,128)(2,1)} %recovery.1, s32[4,2048]{1,0:T(4,128)} %whole.1), custom_call_target="tpu_custom_call" | custom-call | flops 10000000000 | bytes 10000000 | tf_op jit(solution)/shard_map/stress/pallas_call | solution.py:227
  31.1 2.6 %collective-permute-start = (bf16[32,384]{1,0:T(8,128)(2,1)}, bf16[32,384]{1,0:T(8,128)(2,1)S(1)}, u32[]{:S(2)}, u32[]{:S(2)}) collective-permute-start(bf16[32,384]{1,0:T(8,128)(2,1)} %get-tuple-element.15), channel_id=1, source_target_pairs={{0,16},{16,32},{32,48},{48,64},{64,80},{80,96},{96,112},{112,0},{1... | collective-permute-start | bytes 73736 | tf_op jit(solution)/shard_map/ppermute | solution.py:209
  33.7 0.0 collective-permute-start.1
  33.7 1.6 %collective-permute-start.2 = (bf16[32,384]{1,0:T(8,128)(2,1)}, bf16[32,384]{1,0:T(8,128)(2,1)S(1)}, u32[]{:S(2)}, u32[]{:S(2)}) collective-permute-start(bf16[32,384]{1,0:T(8,128)(2,1)} %get-tuple-element.17), channel_id=1, source_target_pairs={{0,1},{1,2},{2,3},{3,4},{4,5},{5,6},{6,7},{7,8},{8,9},{9,10},{10,1... | collective-permute-start | bytes 73736 | tf_op jit(solution)/shard_map/ppermute | solution.py:209
  35.3 4.6 %collective-permute-start.3 = (bf16[32,384]{1,0:T(8,128)(2,1)}, bf16[32,384]{1,0:T(8,128)(2,1)S(1)}, u32[]{:S(2)}, u32[]{:S(2)}) collective-permute-start(bf16[32,384]{1,0:T(8,128)(2,1)} %get-tuple-element.18), channel_id=1, source_target_pairs={{0,15},{1,0},{2,1},{3,2},{4,3},{5,4},{6,5},{7,6},{8,7},{9,8},{10,9... | collective-permute-start | bytes 73736 | tf_op jit(solution)/shard_map/ppermute | solution.py:209
  39.9 0.0 copy-start
  39.9 14.5 %scatter.1 = (f32[4,56,512]{2,1,0:T(8,128)}, s32[4,512]{1,0:T(4,128)}) custom-call(bf16[24,48,2048]{2,1,0:T(8,128)(2,1)} %get-tuple-element.12.stress, s32[4,2048]{1,0:T(4,128)} %whole.1, s32[4,2048]{1,0:T(4,128)} %whole.1, s32[1,512]{1,0:T(1,128)} %bitcast.8, f32[24,512]{1,0:T(8,128)} %weights.3), custom_call_target="tpu_custom_call" | custom-call | flops 10000000000 | bytes 10000000 | tf_op jit(solution)/shard_map/scatter/pallas_call | solution.py:255
  54.3 0.0 collective-permute-done.got_w
  54.3 0.0 copy-start.1
  54.4 0.0 collective-permute-done.1.got_e
  54.4 0.0 copy-start.2
  54.4 0.0 collective-permute-done.2.got_s
  54.4 0.0 copy-start.3
  54.4 0.0 collective-permute-done.3.got_n
  54.4 0.0 copy-start.4
  54.4 0.5 copy-done.1
  55.0 0.0 copy-done.2
  55.0 0.0 copy-done.3
  55.0 0.0 copy-done.4
  55.0 3.0 %readout.1 = bf16[1024,128]{1,0:T(8,128)(2,1)} custom-call(f32[4,56,512]{2,1,0:T(8,128)} %get-tuple-element.13.near, s32[4,512]{1,0:T(4,128)} %get-tuple-element.14.ids, bf16[32,384]{1,0:T(8,128)(2,1)} %copy-done.1, bf16[32,384]{1,0:T(8,128)(2,1)} %copy-done.2, bf16[32,384]{1,0:T(8,128)(2,1)} %copy-done.3, bf16[32,384]{1,0:T(8,128)(2,1)} %copy-done.4, ...), custom_call_target="tpu_custom_call" | custom-call | tf_op jit(solution)/shard_map/readout/pallas_call | solution.py:278
  58.0 17.7 %all_to_all.5 = bf16[128,8,128]{2,1,0:T(8,128)(2,1)S(1)} all-to-all(bf16[128,8,128]{2,1,0:T(8,128)(2,1)} %bitcast.6), channel_id=1, replica_groups=mesh['px'=8,'py'=16] {'px','py'}, dimensions={0} | all-to-all | bytes 524288 | tf_op jit(solution)/shard_map/all_to_all | solution.py:286
  75.7 0.0 copy-done
  75.7 1.5 %convolution_convert_fusion = bf16[1024,576]{0,1:T(8,128)(2,1)} fusion(bf16[128,8,128]{2,1,0:T(8,128)(2,1)S(1)} %all_to_all.5, bf16[48,576]{1,0:T(8,128)(2,1)S(1)} %copy-done), kind=kOutput, calls=%fused_computation | convolution fusion | flops 151584768 | bytes 1497088 | tf_op jit(solution)/shard_map/dot_general | solution.py:290
Async XLA Ops:
  31.1 23.3 %collective-permute-start = (bf16[32,384]{1,0:T(8,128)(2,1)}, bf16[32,384]{1,0:T(8,128)(2,1)S(1)}, u32[]{:S(2)}, u32[]{:S(2)}) collective-permute-start(bf16[32,384]{1,0:T(8,128)(2,1)} %get-tuple-element.15), channel_id=1, source_target_pairs={{0,16},{16,32},{32,48},{48,64},{64,80},{80,96},{96,112},{112,0},{1... | collective-permute-start | bytes 73736 | tf_op jit(solution)/shard_map/ppermute | solution.py:209
  33.7 20.7 %collective-permute-start.1 = (bf16[32,384]{1,0:T(8,128)(2,1)}, bf16[32,384]{1,0:T(8,128)(2,1)S(1)}, u32[]{:S(2)}, u32[]{:S(2)}) collective-permute-start(bf16[32,384]{1,0:T(8,128)(2,1)} %get-tuple-element.16), channel_id=1, source_target_pairs={{0,112},{16,0},{32,16},{48,32},{64,48},{80,64},{96,80},{112,96},{1... | collective-permute-start | bytes 73736 | tf_op jit(solution)/shard_map/ppermute | solution.py:209
  33.7 20.7 %collective-permute-start.2 = (bf16[32,384]{1,0:T(8,128)(2,1)}, bf16[32,384]{1,0:T(8,128)(2,1)S(1)}, u32[]{:S(2)}, u32[]{:S(2)}) collective-permute-start(bf16[32,384]{1,0:T(8,128)(2,1)} %get-tuple-element.17), channel_id=1, source_target_pairs={{0,1},{1,2},{2,3},{3,4},{4,5},{5,6},{6,7},{7,8},{8,9},{9,10},{10,1... | collective-permute-start | bytes 73736 | tf_op jit(solution)/shard_map/ppermute | solution.py:209
  35.3 19.1 %collective-permute-start.3 = (bf16[32,384]{1,0:T(8,128)(2,1)}, bf16[32,384]{1,0:T(8,128)(2,1)S(1)}, u32[]{:S(2)}, u32[]{:S(2)}) collective-permute-start(bf16[32,384]{1,0:T(8,128)(2,1)} %get-tuple-element.18), channel_id=1, source_target_pairs={{0,15},{1,0},{2,1},{3,2},{4,3},{5,4},{6,5},{7,6},{8,7},{9,8},{10,9... | collective-permute-start | bytes 73736 | tf_op jit(solution)/shard_map/ppermute | solution.py:209
  39.9 35.8 %copy-start = (bf16[48,576]{1,0:T(8,128)(2,1)S(1)}, bf16[48,576]{1,0:T(8,128)(2,1)}, u32[]{:S(2)}) copy-start(bf16[48,576]{1,0:T(8,128)(2,1)} %param.13) | copy-start | bytes 165892
  54.3 0.6 copy-start.1
  54.4 0.6 copy-start.2
  54.4 0.6 copy-start.3
  54.4 0.6 copy-start.4
